TPU v7x, 128 devices: a whole 4x4x4 slice. The times are simulated.
128 devices in a mesh: gx: 8 (over z, core), gy: 16 (over x, y).
Axes of the slice: x: 4, y: 4, z: 4, core: 2. Of those that a mesh axis runs over, the one named last changes fastest.
Arguments:
- sources: float32 [2, 2048, 2048], P(None, 'gx', 'gy'), may hold values from -4 to 4
- metric: float32 [2048, 2048], P('gx', 'gy'), may hold values from 0.6 to 1.5
- helm: float32 [2048, 2048], P('gx', 'gy'), may hold values from 0.002 to 0.02
Outputs:
- solution: float32 [2, 2048, 2048], P(None, 'gx', 'gy')
- resid: float32 [2, 2048, 2048], P(None, 'gx', 'gy')
All inputs are finite; a program needn't handle non-finite values.
Results may differ from a plain program's by a relative error of at most 0.0009.
Values sent between devices are 32-bit elements; how exact they have to be, the bound alone decides.
No kernel may reach another device: no remote copies, remote signals or barrier semaphores. Data moves between devices by JAX's collectives and lax.ppermute only.
A program may use at most 128 MiB of HBM per device.

v0:
```python
import math

import jax
import jax.numpy as jnp
from jax import lax
from jax.sharding import PartitionSpec as P

ITERS = 2


shift = 0.001


def extended(array, sides, width):
    for axis, dim in sides:
        count, length = (lax.axis_size(axis), array.shape[dim])
        up = [(i, (i + 1) % count) for i in range(count - 1)]
        down = [(j, i) for i, j in up]
        last = lax.slice_in_dim(array, length - width, length, axis=dim)
        leading = lax.slice_in_dim(array, 0, width, axis=dim)
        before = lax.ppermute(last, axis, up)
        after = lax.ppermute(leading, axis, down)
        array = jnp.concatenate([before, array, after], axis=dim)
    return array


def cosine_table(freq, space, length):
    phase = freq * (2 * space + 1) % (4 * length)
    angle = phase.astype(jnp.float32) * (math.pi / (2 * length))
    scale = jnp.where(freq == 0, math.sqrt(1.0 / length), math.sqrt(2.0 / length))
    return scale * jnp.cos(angle)


def eigen(index, length):
    return 2.0 - 2.0 * jnp.cos(index.astype(jnp.float32) * (math.pi / length))


def per_device(sources, metric, helm):
    exact = lax.Precision.HIGHEST
    rows_here = sources.shape[1]
    cols_here = sources.shape[2]
    total_x = rows_here * lax.axis_size("gx")
    total_y = cols_here * lax.axis_size("gy")
    index_x = lax.axis_index("gx") * rows_here + jnp.arange(rows_here, dtype=jnp.int32)
    index_y = lax.axis_index("gy") * cols_here + jnp.arange(cols_here, dtype=jnp.int32)
    every_x = jnp.arange(total_x, dtype=jnp.int32)
    every_y = jnp.arange(total_y, dtype=jnp.int32)
    edge_x = jnp.where(index_x == 0, 1.0, 0.0) + jnp.where(index_x == total_x - 1, 1.0, 0.0)
    edge_y = jnp.where(index_y == 0, 1.0, 0.0) + jnp.where(index_y == total_y - 1, 1.0, 0.0)
    degree = 4.0 - edge_x[:, None] - edge_y[None, :]
    denom = eigen(index_x, total_x)[:, None] + eigen(index_y, total_y)[None, :] + shift
    forward_x = cosine_table(index_x[:, None], every_x[None, :], total_x)
    inverse_x = cosine_table(every_x[:, None], index_x[None, :], total_x)
    forward_y = cosine_table(index_y[:, None], every_y[None, :], total_y)
    inverse_y = cosine_table(every_y[:, None], index_y[None, :], total_y)

    def along_x(data, inverse):

        def fold(total, piece, start):
            if inverse:
                table = inverse_x
                return jnp.einsum("kx,fkj->fxj", table, piece, precision=exact)
            table = forward_x
            return jnp.einsum("kx,fxj->fkj", table, piece, precision=exact)

        empty = jnp.zeros(data.shape, jnp.float32)
        return fold(empty, lax.all_gather(data, "gx", axis=1, tiled=True), jnp.int32(0))

    def along_y(data, inverse):

        def fold(total, piece, start):
            if inverse:
                table = inverse_y
                return jnp.einsum("fil,ly->fiy", piece, table, precision=exact)
            table = forward_y
            return jnp.einsum("fiy,ly->fil", piece, table, precision=exact)

        empty = jnp.zeros(data.shape, jnp.float32)
        return fold(empty, lax.all_gather(data, "gy", axis=2, tiled=True), jnp.int32(0))

    def precondition(resid):
        scaled = resid / metric
        first = along_x(scaled, False)
        second = along_y(first, False)
        third = second / denom
        fourth = along_y(third, True)
        fifth = along_x(fourth, True)
        return fifth / metric

    def norm_sum(resid, direct):
        return lax.psum(jnp.sum(resid * direct, axis=(1, 2)), ("gx", "gy"))

    solution = jnp.zeros_like(sources)
    resid = sources
    direct = precondition(resid)
    search = direct
    gamma = norm_sum(resid, direct)
    for step in range(ITERS):
        weighted = metric * search
        padded = extended(weighted, (("gx", 1), ("gy", 2)), 1)
        beside = padded[:, 2:, 1:-1] + padded[:, :-2, 1:-1]
        beside = beside + padded[:, 1:-1, 2:] + padded[:, 1:-1, :-2]
        image = metric * (degree * weighted - beside) + helm * search
        alpha = gamma / lax.psum(jnp.sum(search * image, axis=(1, 2)), ("gx", "gy"))
        solution = solution + alpha[:, None, None] * search
        resid = resid - alpha[:, None, None] * image
        if step + 1 < ITERS:
            direct = precondition(resid)
            fresh = norm_sum(resid, direct)
            search = direct + (fresh / gamma)[:, None, None] * search
            gamma = fresh
    return (solution, resid)


def solution(mesh):
    in_specs = (P(None, "gx", "gy"), P("gx", "gy"), P("gx", "gy"))
    out_specs = (P(None, "gx", "gy"), P(None, "gx", "gy"))
    return jax.shard_map(
        per_device, mesh=mesh, in_specs=in_specs, out_specs=out_specs, check_vma=False
    )
```

profile of v0, /device:TPU:0, one launch (start us, length us, event | category | flops | bytes accessed | tf_op | source)
XLA Modules:
  0.0 667.4 jit_solution(12419001002792071462)
XLA Ops:
  7.2 1.0 copy.5
  8.2 1.1 copy.7
  9.3 0.7 broadcast_divide_fusion.1
  10.2 28.0 %all-gather.9.cloned.1.call-done = f32[2,2048,128]{1,2,0:T(8,128)} async-done(((f32[2,256,128]{1,2,0:T(8,128)}), f32[2,2048,128]{1,2,0:T(8,128)}) %all-gather.9.cloned.1.call-update) | async-done | bytes 2097168 | tf_op jit(solution)/shard_map/all_gather | solution.py:67
  38.2 11.8 %fusion.23 = f32[2,256,128]{1,2,0:T(8,128)} fusion(f32[2,2048,128]{1,2,0:T(8,128)} %all-gather.9.cloned.1.call-done, s32[2048]{0:T(1024)S(1)} %multiply_add_fusion.2, s32[256]{0:T(256)S(1)} %iota_add_fusion, f32[256]{0:T(256)S(1)} %fusion.130), kind=kOutput, calls=%fused_computation.35 | convolution fusion | flops 1618477056 | bytes 2369536 | tf_op jit(solution)/shard_map/kx,fxj->fkj/dot_general | solution.py:64
  50.0 0.2 all-gather.13.cloned.1.call-start
  50.4 0.1 add_add_fusion
  50.5 51.5 %all-gather.11.cloned.1.call-done = f32[2,256,2048]{1,2,0:T(8,128)} async-done(((f32[2,256,128]{1,2,0:T(8,128)}), f32[2,256,2048]{1,2,0:T(8,128)}) %all-gather.11.cloned.1.call-update) | async-done | bytes 4194320 | tf_op jit(solution)/shard_map/all_gather | solution.py:79
  102.0 13.1 %convolution_divide_fusion.1 = f32[2,256,128]{2,1,0:T(8,128)} fusion(f32[2,256,2048]{1,2,0:T(8,128)} %all-gather.11.cloned.1.call-done, s32[2048]{0:T(1024)S(1)} %multiply_add_fusion.2, s32[128]{0:T(128)S(1)} %iota_add_fusion.1, f32[128]{0:T(128)S(1)} %get-tuple-element.29, f32[256,128]{1,0:T(8,128)S(1)} %add_add_fusion), kind=kOutput, calls=%fused_computation.40 | convolution fusion | flops 1614610432 | bytes 4596736 | tf_op jit(solution)/shard_map/fiy,ly->fil/dot_general | solution.py:76
  115.1 0.3 all-gather.15.cloned.1.call-start
  115.4 57.0 %all-gather.13.cloned.1.call-done = f32[2,256,2048]{2,1,0:T(8,128)} async-done(((f32[2,256,128]{2,1,0:T(8,128)}), f32[2,256,2048]{2,1,0:T(8,128)}) %all-gather.13.cloned.1.call-update) | async-done | bytes 4194320 | tf_op jit(solution)/shard_map/all_gather | solution.py:79
  172.4 11.2 %fusion.84 = f32[2,256,128]{1,2,0:T(8,128)} fusion(f32[2,256,2048]{2,1,0:T(8,128)} %all-gather.13.cloned.1.call-done, s32[128]{0:T(128)S(1)} %multiply_add_fusion.4, f32[2048]{0:T(1024)S(1)} %fusion.126), kind=kOutput, calls=%fused_computation.85 | convolution fusion | flops 1614544896 | bytes 4465152 | tf_op jit(solution)/shard_map/fil,ly->fiy/dot_general | solution.py:74
  183.6 0.4 all-gather.17.cloned.1.call-start
  184.1 24.5 %all-gather.15.cloned.1.call-done = f32[2,2048,128]{1,2,0:T(8,128)} async-done(((f32[2,256,128]{1,2,0:T(8,128)}), f32[2,2048,128]{1,2,0:T(8,128)}) %all-gather.15.cloned.1.call-update) | async-done | bytes 2097168 | tf_op jit(solution)/shard_map/all_gather | solution.py:67
  208.6 11.1 %broadcast_multiply_fusion.1 = (f32[2,256,128]{1,2,0:T(8,128)S(1)}, f32[2,256,128]{1,2,0:T(8,128)S(1)}) fusion(f32[256,128]{0,1:T(8,128)S(1)} %copy.5, f32[2,2048,128]{1,2,0:T(8,128)} %all-gather.15.cloned.1.call-done, s32[256]{0:T(256)S(1)} %multiply_add_fusion.3, f32[2048]{0:T(1024)S(1)} %fusion.126), kind=kOutput, calls=%fused_computation.151 | convolution fusion | flops 1618608128 | bytes 2761728 | tf_op jit(solution)/shard_map/kx,fkj->fxj/dot_general | solution.py:62
  219.9 2.2 collective-permute-start.1
  222.0 1.3 collective-permute-start
  223.4 1.9 collective-permute-done
  225.4 1.3 collective-permute-start.2
  226.7 4.5 collective-permute-start.3
  231.3 0.1 copy.8
  231.4 1.1 collective-permute-done.3
  232.5 0.4 multiply_reduce_fusion.2
  232.9 71.9 %all-reduce = (f32[2]{0:T(128)S(1)}, f32[2]{0:T(128)S(1)}) all-reduce(f32[2]{0:T(128)S(1)} %get-tuple-element.5, f32[2]{0:T(128)S(1)} %get-tuple-element.4), channel_id=1, replica_groups=mesh['gx'=8,'gy'=16] {'gx','gy'}, use_global_device_ids=true, to_apply=%region_1.2 | all-reduce | flops 4 | bytes 32 | tf_op jit(solution)/shard_map/psum | solution.py:91
  304.9 0.8 broadcast_divide_fusion
  305.8 22.7 %all-gather.17.cloned.1.call-done = f32[2,2048,128]{1,2,0:T(8,128)} async-done(((f32[2,256,128]{1,2,0:T(8,128)}), f32[2,2048,128]{1,2,0:T(8,128)}) %all-gather.17.cloned.1.call-update) | async-done | bytes 2097168 | tf_op jit(solution)/shard_map/all_gather | solution.py:67
  328.5 11.8 %fusion.26 = f32[2,256,128]{1,2,0:T(8,128)} fusion(f32[2,2048,128]{1,2,0:T(8,128)} %all-gather.17.cloned.1.call-done, s32[2048]{0:T(1024)S(1)} %multiply_add_fusion.2, s32[256]{0:T(256)S(1)} %iota_add_fusion, f32[256]{0:T(256)S(1)} %fusion.130), kind=kOutput, calls=%fused_computation.36 | convolution fusion | flops 1618477056 | bytes 2369536 | tf_op jit(solution)/shard_map/kx,fxj->fkj/dot_general | solution.py:64
  340.4 0.3 all-gather.21.cloned.1.call-start
  340.6 51.7 %all-gather.19.cloned.1.call-done = f32[2,256,2048]{1,2,0:T(8,128)} async-done(((f32[2,256,128]{1,2,0:T(8,128)}), f32[2,256,2048]{1,2,0:T(8,128)}) %all-gather.19.cloned.1.call-update) | async-done | bytes 4194320 | tf_op jit(solution)/shard_map/all_gather | solution.py:79
  392.3 13.1 %convolution_divide_fusion = f32[2,256,128]{2,1,0:T(8,128)} fusion(f32[2,256,2048]{1,2,0:T(8,128)} %all-gather.19.cloned.1.call-done, s32[2048]{0:T(1024)S(1)} %multiply_add_fusion.2, s32[128]{0:T(128)S(1)} %iota_add_fusion.1, f32[128]{0:T(128)S(1)} %get-tuple-element.29, f32[256,128]{1,0:T(8,128)S(1)} %add_add_fusion), kind=kOutput, calls=%fused_computation.39 | convolution fusion | flops 1614610432 | bytes 4596736 | tf_op jit(solution)/shard_map/fiy,ly->fil/dot_general | solution.py:76
  405.5 0.4 all-gather.23.cloned.1.call-start
  405.9 56.8 %all-gather.21.cloned.1.call-done = f32[2,256,2048]{2,1,0:T(8,128)} async-done(((f32[2,256,128]{2,1,0:T(8,128)}), f32[2,256,2048]{2,1,0:T(8,128)}) %all-gather.21.cloned.1.call-update) | async-done | bytes 4194320 | tf_op jit(solution)/shard_map/all_gather | solution.py:79
  462.7 11.2 %fusion.82 = f32[2,256,128]{1,2,0:T(8,128)} fusion(f32[2,256,2048]{2,1,0:T(8,128)} %all-gather.21.cloned.1.call-done, s32[128]{0:T(128)S(1)} %multiply_add_fusion.4, f32[2048]{0:T(1024)S(1)} %fusion.126), kind=kOutput, calls=%fused_computation.84 | convolution fusion | flops 1614544896 | bytes 4465152 | tf_op jit(solution)/shard_map/fil,ly->fiy/dot_general | solution.py:74
  474.0 25.0 %all-gather.23.cloned.1.call-done = f32[2,2048,128]{1,2,0:T(8,128)} async-done(((f32[2,256,128]{1,2,0:T(8,128)}), f32[2,2048,128]{1,2,0:T(8,128)}) %all-gather.23.cloned.1.call-update) | async-done | bytes 2097168 | tf_op jit(solution)/shard_map/all_gather | solution.py:67
  498.9 11.4 %multiply_reduce_fusion.1 = (f32[2]{0:T(128)S(1)}, f32[2,256,128]{1,2,0:T(8,128)S(1)}) fusion(f32[2,256,128]{1,2,0:T(8,128)S(1)} %get-tuple-element.13, f32[256,128]{0,1:T(8,128)S(1)} %copy.5, f32[2,2048,128]{1,2,0:T(8,128)} %all-gather.23.cloned.1.call-done, s32[256]{0:T(256)S(1)} %multiply_add_fusion.3, f32[2048]{0:T(1024)S(1)} %fusion.126), kind=kOutput, calls=%fused_computation.144 | convolution fusion | flops 1618673664 | bytes 2761736 | tf_op jit(solution)/shard_map/kx,fkj->fxj/dot_general | solution.py:62
  510.3 65.4 %psum.30 = f32[2]{0:T(128)S(1)} all-reduce(f32[2]{0:T(128)S(1)} %get-tuple-element.27), channel_id=1, replica_groups=mesh['gx'=8,'gy'=16] {'gx','gy'}, use_global_device_ids=true, to_apply=%region_5.6 | all-reduce | flops 2 | bytes 16 | tf_op jit(solution)/shard_map/psum | solution.py:91
  575.7 0.1 broadcast_multiply_fusion
  575.9 1.8 collective-permute-start.5
  577.7 1.3 collective-permute-start.4
  579.0 2.5 collective-permute-done.4
  581.6 1.3 collective-permute-start.6
  582.9 4.5 collective-permute-start.7
  587.5 1.3 collective-permute-done.7
  588.8 0.4 multiply_reduce_fusion
  589.2 69.3 %psum.31 = f32[2]{0:T(128)S(1)} all-reduce(f32[2]{0:T(128)S(1)} %get-tuple-element.8), channel_id=1, replica_groups=mesh['gx'=8,'gy'=16] {'gx','gy'}, use_global_device_ids=true, to_apply=%region_7.8 | all-reduce | flops 2 | bytes 16 | tf_op jit(solution)/shard_map/psum | solution.py:104
  658.5 0.1 multiply_subtract_fusion
  658.7 0.8 copy.11
  659.5 0.8 copy.10
  (36 shorter events, 0.8 us)
Async XLA Ops:
  7.2 31.0 %all-gather.9.cloned.1.call-start = ((), (), s32[]{:S(2)}) async-start(), calls=%async_computation | async-start | bytes 2359296 | tf_op jit(solution)/shard_map/all_gather | solution.py:67
  10.1 91.9 %all-gather.11.cloned.1.call-start = ((), (), s32[]{:S(2)}) async-start(), calls=%async_computation.1 | async-start | bytes 4456448 | tf_op jit(solution)/shard_map/all_gather | solution.py:79
  50.0 122.4 %all-gather.13.cloned.1.call-start = ((), (), s32[]{:S(2)}) async-start(), calls=%async_computation.2 | async-start | bytes 4456448 | tf_op jit(solution)/shard_map/all_gather | solution.py:79
  115.1 93.5 %all-gather.15.cloned.1.call-start = ((), (), s32[]{:S(2)}) async-start(), calls=%async_computation.3 | async-start | bytes 2359296 | tf_op jit(solution)/shard_map/all_gather | solution.py:67
  183.6 144.9 %all-gather.17.cloned.1.call-start = ((), (), s32[]{:S(2)}) async-start(), calls=%async_computation.4 | async-start | bytes 2359296 | tf_op jit(solution)/shard_map/all_gather | solution.py:67
  184.1 47.2 %copy-start = (f32[256,128]{1,0:T(8,128)S(1)}, f32[256,128]{1,0:T(8,128)}, u32[]{:S(2)}) copy-start(f32[256,128]{1,0:T(8,128)} %param.5) | copy-start | bytes 393220
  219.9 3.5 collective-permute-start.1
  222.0 3.2 collective-permute-start
  225.4 6.1 collective-permute-start.2
  226.7 5.9 collective-permute-start.3
  305.7 86.6 %all-gather.19.cloned.1.call-start = ((), (), s32[]{:S(2)}) async-start(), calls=%async_computation.5 | async-start | bytes 4456448 | tf_op jit(solution)/shard_map/all_gather | solution.py:79
  340.4 122.4 %all-gather.21.cloned.1.call-start = ((), (), s32[]{:S(2)}) async-start(), calls=%async_computation.6 | async-start | bytes 4456448 | tf_op jit(solution)/shard_map/all_gather | solution.py:79
  405.5 93.5 %all-gather.23.cloned.1.call-start = ((), (), s32[]{:S(2)}) async-start(), calls=%async_computation.7 | async-start | bytes 2359296 | tf_op jit(solution)/shard_map/all_gather | solution.py:67
  575.9 3.1 collective-permute-start.5
  577.7 3.8 collective-permute-start.4
  581.6 5.9 collective-permute-start.6
  582.9 5.9 collective-permute-start.7
Sparse Core Ops, SparseCore 0:
  10.3 27.8 all-gather.8
  50.1 51.8 all-gather.10
  115.2 57.1 all-gather.12
  183.8 24.8 all-gather.14
  305.9 22.5 all-gather.16
  340.5 51.8 all-gather.18
  405.6 57.1 all-gather.20
  474.1 24.8 all-gather.22
where the time goes:
time: 676 us; the launch traced here: 667 us
  waiting for transfers between devices  324 us (48%)
  blocking collectives  207 us (31%)
  matrix products  94.8 us (14%)
  starting transfers between devices  19.9 us (3%)
  between operations  14.6 us (2%)
    all_gather x4, waiting for transfers between devices, along_y(): lax.all_gather(data, 'gy', axis=2, tiled=True)  217 us
    psum x2, blocking collectives, norm_sum(): return lax.psum(jnp.sum(resid * direct, axis=(1, 2)), ('gx', 'gy'))  137 us
    all_gather x4, waiting for transfers between devices, along_x(): lax.all_gather(data, 'gx', axis=1, tiled=True)  100 us
    psum x1, blocking collectives, per_device(): alpha = gamma / lax.psum(jnp.sum(search * image, axis=(1, 2)), ('gx', 'gy'))  69.3 us
    dot_general x2, matrix products, fold(): return jnp.einsum('fiy,ly->fil', piece, table, precision=exact)  26.2 us
    dot_general x2, matrix products, fold(): return jnp.einsum('kx,fxj->fkj', table, piece, precision=exact)  23.7 us
    dot_general x2, matrix products, fold(): return jnp.einsum('kx,fkj->fxj', table, piece, precision=exact)  22.5 us
    dot_general x2, matrix products, fold(): return jnp.einsum('fil,ly->fiy', piece, table, precision=exact)  22.4 us
  transfers between devices with their start and end apart: 16, of which 12 were waited for; matrix products, arithmetic and copies ran while one was open for 0% of the time, Pallas kernels for 0%

commit v1 on v0

v1 whole, which is shorter than its diff:
```python
import functools
import math

import jax
import jax.numpy as jnp
import ml_dtypes
import numpy as np
from jax import lax
from jax.experimental import pallas as pl
from jax.experimental.pallas import tpu as pltpu
from jax.sharding import PartitionSpec as P

SHIFT = 0.001
ROWS = 16
LANES = 128
LENGTH = ROWS * LANES


def frequency():
    t = np.arange(16)[:, None]
    k2 = np.arange(64)[None, :]
    first = t + 32 * k2
    second = np.where(t == 0, 16, 32 - t) + 32 * k2
    return np.concatenate([first, second], axis=1)


def tables():
    freq = frequency()
    b = np.arange(LANES)
    phase = (freq[:, None, :] * (2 * b[None, :, None] + 1)) % (4 * LENGTH)
    angle = phase * (math.pi / (2 * LENGTH))
    scale = np.where(freq == 0, math.sqrt(1.0 / LENGTH), math.sqrt(2.0 / LENGTH))[:, None, :]
    even, odd = scale * np.cos(angle), scale * np.sin(angle)
    sign = np.where(np.arange(LANES) < 64, -1.0, 1.0)
    full = np.concatenate([even, odd * sign], axis=1)
    full[0, :LANES, 64:] = 0.0
    full[0, LANES:, :64] = 0.0
    full[0, LANES:, 64:] = even[0, :, 64:]
    beside = np.concatenate([full[:, :LANES], full[:, LANES:]], axis=2)
    full = np.concatenate([np.swapaxes(full, 1, 2), beside], axis=1)
    high = full.astype(ml_dtypes.bfloat16)
    low = (full - high.astype(np.float64)).astype(ml_dtypes.bfloat16)
    lam = 4.0 * np.sin(math.pi * freq / (2 * LENGTH)) ** 2
    return np.stack([high, low], axis=1), lam.astype(np.float32)


def cos16(n):
    return float(math.cos(math.pi * n / 16))


def sin16(n):
    return float(math.sin(math.pi * n / 16))


def combine(terms):
    total = None
    for c, v in terms:
        if abs(c) < 1e-12:
            continue
        if abs(abs(c) - 1.0) < 1e-12:
            if total is None:
                total = v if c > 0 else -v
            else:
                total = total + v if c > 0 else total - v
        else:
            total = c * v if total is None else total + c * v
    return total


def first_stage(x):
    p = {a: x[a] + x[16 - a] for a in range(1, 8)}
    m = {a: x[a] - x[16 - a] for a in range(1, 8)}
    R, S = {}, {}
    for j in range(1, 8):
        c, s = (m, p) if j % 2 else (p, m)
        ev = combine([(1.0, x[0])] + [(cos16(j * a), c[a]) for a in (2, 4, 6)] + [(cos16(8 * j), x[8])])
        od = combine([(cos16(j * a), c[a]) for a in (1, 3, 5, 7)])
        R[j], R[16 - j] = ev + od, ev - od
        ev = combine([(sin16(j * a), s[a]) for a in (2, 4, 6)] + [(sin16(8 * j), x[8])])
        od = combine([(sin16(j * a), s[a]) for a in (1, 3, 5, 7)])
        S[j], S[16 - j] = od + ev, od - ev
    outer, inner = x[0] + x[8], p[2] + p[6]
    R[8] = outer + p[4] - inner
    S[8] = (m[1] + m[5]) - (m[3] + m[7])
    even, odd = outer + p[4] + inner, (p[1] + p[7]) + (p[3] + p[5])
    R[0], R[16] = even + odd, even - odd
    return R, S


def first_stage_transposed(R, S):
    rp = {j: R[j] + R[16 - j] for j in range(1, 8)}
    rm = {j: R[j] - R[16 - j] for j in range(1, 8)}
    sp = {j: S[j] + S[16 - j] for j in range(1, 8)}
    sm = {j: S[j] - S[16 - j] for j in range(1, 8)}
    ends, wide = R[0] + R[16], R[0] - R[16]
    x = {}
    for a in range(1, 8):
        r, s = (rm, sp) if a % 2 else (rp, sm)
        ce = combine([(1.0, wide if a % 2 else ends), (cos16(8 * a), R[8])] + [(cos16(j * a), r[j]) for j in (2, 4, 6)])
        co = combine([(cos16(j * a), r[j]) for j in (1, 3, 5, 7)])
        se = combine([(sin16(8 * a), S[8])] + [(sin16(j * a), s[j]) for j in (2, 4, 6)])
        so = combine([(sin16(j * a), s[j]) for j in (1, 3, 5, 7)])
        x[a], x[16 - a] = (ce + so) + (co + se), (ce + so) - (co + se)
    even = ends + R[8] + rp[2] + rp[4] + rp[6]
    x[0] = even + (rp[1] + rp[7]) + (rp[3] + rp[5])
    x[8] = ends + R[8] - rp[2] + rp[4] - rp[6] + (sm[1] - sm[3]) + (sm[5] - sm[7])
    return x


def split_dot(value, high_table, low_table):
    rows = value.shape[0]
    high = value.astype(jnp.bfloat16)
    low = (value - high.astype(jnp.float32)).astype(jnp.bfloat16)
    both = jnp.dot(jnp.concatenate([high, low], axis=0), high_table, preferred_element_type=jnp.float32)
    third = jnp.dot(high, low_table, preferred_element_type=jnp.float32)
    return both[:rows] + (both[rows:] + third)


def forward_dot(value, table, t):
    halves = [[table[t, n, LANES:, LANES * k : LANES * (k + 1)] for k in range(2)] for n in range(2)]
    return split_dot(value, *[jnp.concatenate(pair, axis=0) for pair in halves])


def backward_dot(value, table, t):
    return split_dot(value, table[t, 0, :LANES, :], table[t, 1, :LANES, :])


def put_first(R, S, rs, chunk):
    rows = pl.ds(8 * chunk, 8)
    for t in range(16):
        rs[t, rows, 0:LANES] = R[t]
        rs[t, rows, LANES : 2 * LANES] = R[16] if t == 0 else S[t]


def get_first(rs, chunk):
    rows = pl.ds(8 * chunk, 8)
    R = {t: rs[t, rows, 0:LANES] for t in range(16)}
    S = {t: rs[t, rows, LANES : 2 * LANES] for t in range(1, 16)}
    R[16] = rs[0, rows, LANES : 2 * LANES]
    return R, S


def leave_block(
    sources, metric, helm, table, lam, columns, here, fields, weights, factors, source_here, metric_here, helm_here, arrived
):
    moves = [(metric, metric_here), (sources.at[0], source_here.at[0]), (sources.at[1], source_here.at[1]), (helm, helm_here)]
    copies = [pltpu.make_async_copy(a, b, arrived.at[n]) for n, (a, b) in enumerate(moves)]
    for copy in copies:
        copy.start()
    lane = lax.broadcasted_iota(jnp.int32, (32, LANES), 1)
    mine = jnp.sum(jnp.where(lane == here[...], columns[...], 0.0), axis=1, keepdims=True)
    for t in range(16):
        factors[t] = 1.0 / (mine + (lam[pl.ds(t, 1), :] + SHIFT))
    copies[0].wait()
    inverse = 1.0 / metric_here[...]
    for f in range(2):
        copies[1 + f].wait()
        field = source_here[f] * inverse
        for h in range(2):
            across = field[LANES * h : LANES * (h + 1), :].T
            for peer in range(8):
                fields[pl.ds(64 * peer + 32 * f + h, 16, stride=2), :] = across[16 * peer : 16 * (peer + 1)]
    copies[3].wait()
    weight = helm_here[...] * (inverse * inverse) - SHIFT
    for h in range(2):
        across = weight[LANES * h : LANES * (h + 1), :].T
        for g in range(2):
            weights[pl.ds(2 * g + h, 64, stride=4), :] = across[64 * g : 64 * (g + 1)]


def pencil_x_first(fields, own, table, sent, rs, flat):
    for chunk in range(4):
        x = [fields[pl.ds(64 * (a // 2) + 16 * chunk + a % 2, 8, stride=2), :] for a in range(16)]
        put_first(*first_stage(x), rs, chunk)
    for n in range(4):
        weight = own[pl.ds(n, 64, stride=4), :]
        for f in range(2):
            sent[pl.ds(512 * f + 2 * n + 1, 64, stride=8), :] = weight
    forward_along_x(table, rs, flat)
    for f in range(2):
        for u in range(2):
            across = flat[pl.ds(256 * f + LANES * u, LANES), :].T
            for s in range(2):
                sent[pl.ds(512 * f + 2 * (2 * s + u), 64, stride=8), :] = across[64 * s : 64 * (s + 1)]


def forward_along_x(table, rs, flat):
    for t in range(16):
        lines = forward_dot(rs[t], table, t)
        for g in range(2):
            flat[pl.ds(256 * g + 16 * t, 16), :] = lines[16 * g : 16 * (g + 1)]


def along_y(table, factors, sent, rs, flat):
    for chunk in range(4):
        x = [flat[pl.ds(LANES * chunk + a, 8, stride=16), :] for a in range(16)]
        put_first(*first_stage(x), rs, chunk)
    total = jnp.zeros((32, LANES), jnp.float32)
    for t in range(16):
        spectrum = forward_dot(rs[t], table, t)
        scaled = spectrum * factors[t]
        total += spectrum * scaled
        rs[t] = backward_dot(scaled, table, t)
    for chunk in range(4):
        x = first_stage_transposed(*get_first(rs, chunk))
        for a in range(16):
            flat[pl.ds(LANES * chunk + a, 8, stride=16), :] = x[a]
    for r in range(4):
        across = flat[pl.ds(LANES * r, LANES), :].T
        for g in range(2):
            sent[pl.ds(4 * g + r, 64, stride=8), :] = across[64 * g : 64 * (g + 1)]
    return (total[0:8] + total[8:16]) + (total[16:24] + total[24:32])


def pencil_y_first(received, table, factors, sent, total, rs, flat):
    lane = lax.broadcasted_iota(jnp.int32, (8, LANES), 1)
    for pair in range(8):
        v = [received[pl.ds((16 * i + 2 * pair) * 8, 8, stride=2), :] for i in range(8)]
        for step in (4, 2, 1):
            upper = (lane // (16 * step)) % 2 == 1
            w = list(v)
            for i in range(8):
                if not i & step:
                    w[i] = jnp.where(upper, pltpu.roll(v[i + step], 16 * step, 1), v[i])
                    w[i + step] = jnp.where(upper, v[i + step], pltpu.roll(v[i], LANES - 16 * step, 1))
            v = w
        for n in range(8):
            for m in range(2):
                flat[pl.ds(16 * n + 2 * pair + m, 4, stride=LANES), :] = v[n][4 * m : 4 * (m + 1)]
    total[...] = along_y(table, factors, sent, rs, flat)


def pencil_y_second(received, table, factors, sent, rs, flat):
    for r in range(4):
        lines = [received[pl.ds(4 * g + r, 64, stride=8), :] for g in range(2)]
        flat[pl.ds(LANES * r, LANES), :] = jnp.concatenate(lines, axis=0).T
    along_y(table, factors, sent, rs, flat)


def weight_at(weights, a, chunk):
    g, half = chunk // 2, chunk % 2
    start = (16 * (a // 2) + 8 * half) * 8 + 2 * (2 * g + a % 2) + 1
    return weights[pl.ds(start, 8, stride=8), :]


def back_along_x(received, table, rs, flat):
    for g in range(2):
        for u in range(2):
            lines = [received[pl.ds(4 * g + 2 * s + u, 64, stride=8), :] for s in range(2)]
            flat[pl.ds(256 * g + LANES * u, LANES), :] = jnp.concatenate(lines, axis=0).T
    for t in range(16):
        both = [flat[pl.ds(256 * g + 16 * t, 16), :] for g in range(2)]
        rs[t] = backward_dot(jnp.concatenate(both, axis=0), table, t)


def pencil_x_middle(received, weights, table, sent, kept, rs, flat):
    back_along_x(received, table, rs, flat)
    for chunk in range(4):
        x = first_stage_transposed(*get_first(rs, chunk))
        for a in range(16):
            kept[a, pl.ds(8 * chunk, 8), :] = x[a]
        x = [x[a] * weight_at(weights, a, chunk) for a in range(16)]
        put_first(*first_stage(x), rs, chunk)
    forward_along_x(table, rs, flat)
    for g in range(2):
        for u in range(2):
            across = flat[pl.ds(256 * g + LANES * u, LANES), :].T
            for s in range(2):
                sent[pl.ds(4 * g + 2 * s + u, 64, stride=8), :] = across[64 * s : 64 * (s + 1)]


def pencil_x_last(received, weights, kept, total, table, sent, rs, flat):
    back_along_x(received, table, rs, flat)
    sums = [total[...]] + [jnp.zeros((8, LANES), jnp.float32) for _ in range(3)]
    for chunk in range(4):
        x = first_stage_transposed(*get_first(rs, chunk))
        for a in range(16):
            old, new = kept[a, pl.ds(8 * chunk, 8), :], x[a]
            weight = weight_at(weights, a, chunk)
            scaled = weight * old
            sums[1] += scaled * old
            sums[2] += scaled * new
            sums[3] += weight * new * new
            place = ((a // 2) * 16 + 8 * (chunk % 2)) * 9 + 2 * (chunk // 2) + a % 2
            sent[pl.ds(place, 8, stride=9), :] = old
            sent[pl.ds(place + 4, 8, stride=9), :] = new
    lane = lax.broadcasted_iota(jnp.int32, (1, LANES), 1)
    line = jnp.zeros((1, LANES), jnp.float32)
    for q in range(4):
        line = jnp.where(lane == q, jnp.sum(sums[q]), line)
    sent[pl.ds(8, LANES, stride=9), :] = jnp.broadcast_to(line, (LANES, LANES))


def enter_block(received, sources, metric, helm, solution, resid):
    lane = lax.broadcasted_iota(jnp.int32, (1, LANES), 1)
    m = metric[...]
    inverse = 1.0 / m
    weight = helm[...] * inverse - SHIFT * m
    for f in range(2):
        totals = jnp.sum(received[pl.ds(64 * 9 * f + 8, 64, stride=9), :], axis=0, keepdims=True)
        n0, n1, n2, n3 = [
            jnp.sum(jnp.where(lane == q, totals, 0.0), axis=1, keepdims=True) for q in range(4)
        ]
        delta = n0 + n1
        alpha = n0 / delta
        rest = n1 / delta
        gamma = n0 * rest * rest - 2.0 * alpha * rest * n1 + alpha * alpha * n2
        beta = gamma / n0
        p, q = rest + beta, -alpha
        second = gamma / (p * p * delta + 2.0 * p * q * (n1 + n2) + q * q * (n2 + n3))
        c0, c1 = alpha + second * p, second * q
        for h in range(2):
            pair = []
            for field in range(2):
                lines = [
                    received[pl.ds(64 * 9 * f + 4 * field + 2 * g + h, 64, stride=9), :] for g in range(2)
                ]
                pair.append(jnp.concatenate(lines, axis=0).T)
            old, new = pair
            rows = slice(LANES * h, LANES * (h + 1))
            solution[f, rows, :] = (c0 * old + c1 * new) * inverse[rows]
            resid[f, rows, :] = (1.0 - c0) * sources[f, rows, :] - ((c0 + c1) * old + c1 * new) * weight[rows]


RS = pltpu.VMEM((16, 32, 2 * LANES), jnp.float32)
FLAT = pltpu.VMEM((512, LANES), jnp.float32)


def call(kernel, outs, scratch=(RS, FLAT), **more):
    return pl.pallas_call(
        kernel,
        out_shape=[jax.ShapeDtypeStruct(s, jnp.float32) if isinstance(s, tuple) else s for s in outs],
        scratch_shapes=scratch,
        compiler_params=pltpu.CompilerParams(vmem_limit_bytes=32 * 1024 * 1024),
        **more,
    )


def far(*arrays):
    return [pltpu.with_memory_space_constraint(a, pltpu.HBM) for a in arrays]


def exchange(flat, axes, *shape):
    moved = lax.all_to_all(flat.reshape(*shape, LANES), axes, 0, 0, tiled=True)
    return moved.reshape(flat.shape)


def per_device(sources, metric, helm):
    pair, eigen = tables()
    group = ("quarter", "gy")
    here = lax.axis_index("quarter") * lax.axis_size("gy") + lax.axis_index("gy")
    columns = np.zeros((32, LANES), np.float32)
    columns[:, :64] = eigen.reshape(16, 2, 64).transpose(1, 0, 2).reshape(32, 64)

    block = pltpu.VMEM(metric.shape, metric.dtype)
    hbm, vmem = pl.BlockSpec(memory_space=pl.ANY), pl.BlockSpec(memory_space=pltpu.VMEM)
    table = jnp.asarray(pair)
    fields, own, factors = call(
        leave_block,
        [(512, LANES), (256, LANES), (16, 32, LANES)],
        [pltpu.VMEM(sources.shape, sources.dtype), block, block, pltpu.SemaphoreType.DMA((4,))],
        in_specs=[hbm] * 4 + [vmem] * 3,
    )(
        *far(sources, metric, helm, table),
        jnp.asarray(eigen),
        jnp.asarray(columns),
        jnp.full((1, LANES), here, jnp.int32),
    )
    fields = exchange(fields, ("half", "quarter"), 8, 64)
    (sent,) = call(pencil_x_first, [(1024, LANES)])(fields, own, table)
    weights = exchange(sent, ("half", "quarter", "gy"), LANES, 8)
    sent, total = call(pencil_y_first, [(512, LANES), (8, LANES)])(weights, table, factors)
    received = exchange(sent, group, 64, 8)
    sent, kept = call(pencil_x_middle, [(512, LANES), (16, 32, LANES)])(received, weights, table)
    received = exchange(sent, group, 64, 8)
    (sent,) = call(pencil_y_second, [(512, LANES)])(received, table, factors)
    received = exchange(sent, group, 64, 8)
    (sent,) = call(pencil_x_last, [(9 * LANES, LANES)])(received, weights, kept, total, table)
    received = exchange(sent, ("half", "quarter", "gy"), LANES, 9, 1)
    return tuple(call(enter_block, [sources.shape] * 2, ())(received, sources, metric, helm))


def solution(mesh):
    devices = mesh.devices.reshape(2, 4, 16)
    finer = jax.sharding.Mesh(devices, ("half", "quarter", "gy"))
    line = ("half", "quarter")
    in_specs = (P(None, line, "gy"), P(line, "gy"), P(line, "gy"))
    out_specs = (P(None, line, "gy"), P(None, line, "gy"))
    return jax.shard_map(
        per_device, mesh=finer, in_specs=in_specs, out_specs=out_specs, check_vma=False
    )
```

time: 676 us -> 106 us (0.16); the launches traced: 667 us -> 106 us
  waiting for transfers between devices: 324 us -> 0 us
  blocking collectives: 207 us -> 95.2 us
  matrix products: 94.8 us -> 0 us
  starting transfers between devices: 19.9 us -> 0 us
  between operations: 14.6 us -> 0.72 us
  Pallas kernels: 0 us -> 7.91 us
    all_gather x8 -> x0, waiting for transfers between devices: 317 us -> none  [the longest x4 217 us: along_y(): lax.all_gather(data, 'gy', axis=2, tiled=True)]
    psum x3 -> x0, blocking collectives: 207 us -> none  [the longest x2 137 us: norm_sum(): return lax.psum(jnp.sum(resid * direct, axis=(1, 2)), ('gx', 'gy'))]
    all_to_all x0 -> x6, blocking collectives: none -> 95.2 us  [exchange(): moved = lax.all_to_all(flat.reshape(*shape, LANES), axes, 0, 0, tiled=True)]
    dot_general x8 -> x0, matrix products: 94.8 us -> none  [the longest x2 26.2 us: fold(): return jnp.einsum('fiy,ly->fil', piece, table, precision=exact)]
    ppermute x8 -> x0, starting transfers between devices: 18.2 us -> none  [the longest x4 13 us: extended(): before = lax.ppermute(last, axis, up)]
    pallas_call x0 -> x7, Pallas kernels: none -> 7.91 us  [the longest x1 1.59 us: per_device(): call(pencil_y_first, [(512, LANES), (8, LANES)])(weights, table, factors)]
    ppermute x8 -> x0, waiting for transfers between devices: 6.82 us -> none  [the longest x4 4.43 us: extended(): after = lax.ppermute(leading, axis, down)]
  transfers between devices with their start and end apart: 16 -> 0, of which waited for: 12 -> 0; matrix products, arithmetic and copies ran while one was open for 0% -> 0% of each run, Pallas kernels for 0% -> 0%
where the time goes in v1:
time: 106 us
  blocking collectives  95.2 us (90%)
  Pallas kernels  7.91 us (7%)
  local copies, waits for them, and re-layouts  1.8 us (2%)
    all_to_all x6, blocking collectives, exchange(): moved = lax.all_to_all(flat.reshape(*shape, LANES), axes, 0, 0, tiled=True)  95.2 us

profile of v1, /device:TPU:0, one launch (start us, length us, event | category | flops | bytes accessed | tf_op | source)
XLA Modules:
  0.0 105.6 jit_solution(3744690146380105332)
XLA Ops:
  0.6 0.0 copy-start
  0.7 0.0 copy-start.4
  0.7 0.9 copy-done.4
  1.5 0.0 copy-start.5
  1.5 0.9 copy-done.5
  2.4 1.3 %shard_map.77 = (f32[512,128]{1,0:T(8,128)S(1)}, f32[256,128]{1,0:T(8,128)S(1)}, f32[16,32,128]{2,1,0:T(8,128)S(1)}) custom-call(f32[2,256,128]{2,1,0:T(8,128)} %sources.3, f32[256,128]{1,0:T(8,128)} %metric.3, f32[256,128]{1,0:T(8,128)} %helm.3, bf16[16,2,256,256]{3,2,1,0:T(8,128)(2,1)} %constant.17.clone.table, f32[16,128]{1,0:T(8,128)S(1)} %copy-done.5, ...), custom_call_target="tpu_custom_call" | custom-call | tf_op jit(solution)/shard_map/pallas_call | solution.py:358
  3.8 12.7 %all_to_all.30 = f32[8,64,128]{2,1,0:T(8,128)S(1)} all-to-all(f32[8,64,128]{2,1,0:T(8,128)S(1)} %bitcast.23), channel_id=1, replica_groups=mesh['half'=2,'quarter'=4,'gy'=16] {'half','quarter'}, dimensions={0} | all-to-all | bytes 524288 | tf_op jit(solution)/shard_map/all_to_all | solution.py:344
  16.5 0.0 copy-done
  16.5 0.6 shard_map.78
  17.1 21.6 %all_to_all.31 = f32[128,8,128]{2,1,0:T(8,128)S(1)} all-to-all(f32[128,8,128]{2,1,0:T(8,128)S(1)} %bitcast.17), channel_id=1, replica_groups=mesh['half'=2,'quarter'=4,'gy'=16] {'half','quarter','gy'}, dimensions={0} | all-to-all | bytes 1048576 | tf_op jit(solution)/shard_map/all_to_all | solution.py:344
  38.7 1.6 %shard_map.79 = (f32[512,128]{1,0:T(8,128)S(1)}, f32[8,128]{1,0:T(8,128)S(1)}) custom-call(f32[1024,128]{1,0:T(8,128)S(1)} %bitcast.12, bf16[16,2,256,256]{3,2,1,0:T(8,128)(2,1)S(1)} %copy-done, f32[16,32,128]{2,1,0:T(8,128)S(1)} %get-tuple-element.11.factors), custom_call_target="tpu_custom_call" | custom-call | tf_op jit(solution)/shard_map/pallas_call | solution.py:372
  40.3 13.6 %all_to_all.32 = f32[64,8,128]{2,1,0:T(8,128)S(1)} all-to-all(f32[64,8,128]{2,1,0:T(8,128)S(1)} %bitcast.25), channel_id=1, replica_groups=mesh['half'=2,'quarter'=4,'gy'=16] {'quarter','gy'}, dimensions={0} | all-to-all | bytes 524288 | tf_op jit(solution)/shard_map/all_to_all | solution.py:344
  53.9 1.2 %shard_map.80 = (f32[512,128]{1,0:T(8,128)S(1)}, f32[16,32,128]{2,1,0:T(8,128)S(1)}) custom-call(f32[512,128]{1,0:T(8,128)S(1)} %bitcast.19, f32[1024,128]{1,0:T(8,128)S(1)} %bitcast.13, bf16[16,2,256,256]{3,2,1,0:T(8,128)(2,1)S(1)} %copy-done), custom_call_target="tpu_custom_call" | custom-call | tf_op jit(solution)/shard_map/pallas_call | solution.py:374
  55.2 14.0 %all_to_all.33 = f32[64,8,128]{2,1,0:T(8,128)S(1)} all-to-all(f32[64,8,128]{2,1,0:T(8,128)S(1)} %bitcast.24), channel_id=1, replica_groups=mesh['half'=2,'quarter'=4,'gy'=16] {'quarter','gy'}, dimensions={0} | all-to-all | bytes 524288 | tf_op jit(solution)/shard_map/all_to_all | solution.py:344
  69.1 1.3 %shard_map.81 = f32[512,128]{1,0:T(8,128)S(1)} custom-call(f32[512,128]{1,0:T(8,128)S(1)} %bitcast.21, bf16[16,2,256,256]{3,2,1,0:T(8,128)(2,1)S(1)} %copy-done, f32[16,32,128]{2,1,0:T(8,128)S(1)} %get-tuple-element.11.factors), custom_call_target="tpu_custom_call" | custom-call | tf_op jit(solution)/shard_map/pallas_call | solution.py:376
  70.5 0.0 copy-start.1
  70.5 0.0 copy-start.2
  70.5 0.0 copy-start.3
  70.5 14.1 %all_to_all.34 = f32[64,8,128]{2,1,0:T(8,128)S(1)} all-to-all(f32[64,8,128]{2,1,0:T(8,128)S(1)} %bitcast.22), channel_id=1, replica_groups=mesh['half'=2,'quarter'=4,'gy'=16] {'quarter','gy'}, dimensions={0} | all-to-all | bytes 524288 | tf_op jit(solution)/shard_map/all_to_all | solution.py:344
  84.6 0.8 shard_map.82
  85.4 19.1 %all_to_all.35 = f32[128,9,1,128]{3,2,1,0:T(1,128)S(1)} all-to-all(f32[128,9,1,128]{3,2,1,0:T(1,128)S(1)} %bitcast.15), channel_id=1, replica_groups=mesh['half'=2,'quarter'=4,'gy'=16] {'half','quarter','gy'}, dimensions={0} | all-to-all | bytes 1179648 | tf_op jit(solution)/shard_map/all_to_all | solution.py:344
  104.6 0.0 copy-done.1
  104.6 0.0 copy-done.2
  104.6 0.0 copy-done.3
  104.6 1.0 shard_map.83
  (1 shorter events, 0.0 us)
Async XLA Ops:
  0.6 15.9 %copy-start = (bf16[16,2,256,256]{3,2,1,0:T(8,128)(2,1)S(1)}, bf16[16,2,256,256]{3,2,1,0:T(8,128)(2,1)}, u32[]{:S(2)}) copy-start(bf16[16,2,256,256]{3,2,1,0:T(8,128)(2,1)} %constant.17.clone.table) | copy-start | bytes 12582916
  0.7 0.9 copy-start.4
  1.5 0.9 copy-start.5
  70.5 34.1 %copy-start.1 = (f32[2,256,128]{2,1,0:T(8,128)S(1)}, f32[2,256,128]{2,1,0:T(8,128)}, u32[]{:S(2)}) copy-start(f32[2,256,128]{2,1,0:T(8,128)} %sources.3) | copy-start | bytes 786436
  70.5 34.1 %copy-start.2 = (f32[256,128]{1,0:T(8,128)S(1)}, f32[256,128]{1,0:T(8,128)}, u32[]{:S(2)}) copy-start(f32[256,128]{1,0:T(8,128)} %metric.3) | copy-start | bytes 393220
  70.5 34.1 %copy-start.3 = (f32[256,128]{1,0:T(8,128)S(1)}, f32[256,128]{1,0:T(8,128)}, u32[]{:S(2)}) copy-start(f32[256,128]{1,0:T(8,128)} %helm.3) | copy-start | bytes 393220

commit v2 on v1

v2 whole, which is shorter than its diff:
```python
import functools
import math

import jax
import jax.numpy as jnp
import ml_dtypes
import numpy as np
from jax import lax
from jax.experimental import pallas as pl
from jax.experimental.pallas import tpu as pltpu
from jax.sharding import PartitionSpec as P

SHIFT = 0.001
ROWS = 16
BLOCK = 32
BLOCKS = 64
LANES = 128
LENGTH = ROWS * LANES


def frequency():
    t = np.arange(16)[:, None]
    k2 = np.arange(64)[None, :]
    first = t + 32 * k2
    second = np.where(t == 0, 16, 32 - t) + 32 * k2
    return np.concatenate([first, second], axis=1)


def tables():
    freq = frequency()
    b = np.arange(LANES)
    phase = (freq[:, None, :] * (2 * b[None, :, None] + 1)) % (4 * LENGTH)
    angle = phase * (math.pi / (2 * LENGTH))
    scale = np.where(freq == 0, math.sqrt(1.0 / LENGTH), math.sqrt(2.0 / LENGTH))[:, None, :]
    even, odd = scale * np.cos(angle), scale * np.sin(angle)
    sign = np.where(np.arange(LANES) < 64, -1.0, 1.0)
    full = np.concatenate([even, odd * sign], axis=1)
    full[0, :LANES, 64:] = 0.0
    full[0, LANES:, :64] = 0.0
    full[0, LANES:, 64:] = even[0, :, 64:]
    high = full.astype(ml_dtypes.bfloat16)
    low = (full - high.astype(np.float64)).astype(ml_dtypes.bfloat16)
    forward = np.concatenate([high, low], axis=2)
    sigma = 4.0 * np.sin(math.pi * freq / (2 * LENGTH)) ** 2 + SHIFT
    mu = 2.0 * np.arcsinh(np.sqrt(sigma) / 2.0)
    waves = [np.exp(-mu), BLOCK * mu, 0.5 / np.sinh(mu), 1.0 / (1.0 - np.exp(-2.0 * BLOCK * BLOCKS * mu))]
    return np.stack([forward, np.swapaxes(forward, 1, 2)], axis=1), np.stack(waves).astype(np.float32)


def cos16(n):
    return float(math.cos(math.pi * n / 16))


def sin16(n):
    return float(math.sin(math.pi * n / 16))


def combine(terms):
    total = None
    for c, v in terms:
        if abs(c) < 1e-12:
            continue
        if abs(abs(c) - 1.0) < 1e-12:
            if total is None:
                total = v if c > 0 else -v
            else:
                total = total + v if c > 0 else total - v
        else:
            total = c * v if total is None else total + c * v
    return total


def first_stage(x):
    p = {a: x[a] + x[16 - a] for a in range(1, 8)}
    m = {a: x[a] - x[16 - a] for a in range(1, 8)}
    R, S = {}, {}
    for j in range(1, 8):
        c, s = (m, p) if j % 2 else (p, m)
        ev = combine([(1.0, x[0])] + [(cos16(j * a), c[a]) for a in (2, 4, 6)] + [(cos16(8 * j), x[8])])
        od = combine([(cos16(j * a), c[a]) for a in (1, 3, 5, 7)])
        R[j], R[16 - j] = ev + od, ev - od
        ev = combine([(sin16(j * a), s[a]) for a in (2, 4, 6)] + [(sin16(8 * j), x[8])])
        od = combine([(sin16(j * a), s[a]) for a in (1, 3, 5, 7)])
        S[j], S[16 - j] = od + ev, od - ev
    outer, inner = x[0] + x[8], p[2] + p[6]
    R[8] = outer + p[4] - inner
    S[8] = (m[1] + m[5]) - (m[3] + m[7])
    even, odd = outer + p[4] + inner, (p[1] + p[7]) + (p[3] + p[5])
    R[0], R[16] = even + odd, even - odd
    return R, S


def first_stage_transposed(R, S):
    rp = {j: R[j] + R[16 - j] for j in range(1, 8)}
    rm = {j: R[j] - R[16 - j] for j in range(1, 8)}
    sp = {j: S[j] + S[16 - j] for j in range(1, 8)}
    sm = {j: S[j] - S[16 - j] for j in range(1, 8)}
    ends, wide = R[0] + R[16], R[0] - R[16]
    x = {}
    for a in range(1, 8):
        r, s = (rm, sp) if a % 2 else (rp, sm)
        ce = combine([(1.0, wide if a % 2 else ends), (cos16(8 * a), R[8])] + [(cos16(j * a), r[j]) for j in (2, 4, 6)])
        co = combine([(cos16(j * a), r[j]) for j in (1, 3, 5, 7)])
        se = combine([(sin16(8 * a), S[8])] + [(sin16(j * a), s[j]) for j in (2, 4, 6)])
        so = combine([(sin16(j * a), s[j]) for j in (1, 3, 5, 7)])
        x[a], x[16 - a] = (ce + so) + (co + se), (ce + so) - (co + se)
    even = ends + R[8] + rp[2] + rp[4] + rp[6]
    x[0] = even + (rp[1] + rp[7]) + (rp[3] + rp[5])
    x[8] = ends + R[8] - rp[2] + rp[4] - rp[6] + (sm[1] - sm[3]) + (sm[5] - sm[7])
    return x


def split(value):
    high = value.astype(jnp.bfloat16)
    return high, (value - high.astype(jnp.float32)).astype(jnp.bfloat16)


def forward_dot(value, table, t):
    high, low = split(value)
    both = jnp.dot(jnp.concatenate([high, low], axis=0), table[t, 0, :, :LANES], preferred_element_type=jnp.float32)
    third = jnp.dot(high, table[t, 0, :, LANES:], preferred_element_type=jnp.float32)
    return both[:32] + (both[32:] + third)


def backward_dot(value, table, t):
    high, low = split(value)
    both = jnp.dot(jnp.concatenate([high, low], axis=0), table[t, 1, :LANES, :], preferred_element_type=jnp.float32)
    third = jnp.dot(high, table[t, 1, LANES:, :], preferred_element_type=jnp.float32)
    return both[:32] + (both[32:] + third)


def put_first(R, S, rs, chunk):
    rows = pl.ds(8 * chunk, 8)
    for t in range(16):
        rs[t, rows, 0:LANES] = R[t]
        rs[t, rows, LANES : 2 * LANES] = R[16] if t == 0 else S[t]


def get_first(rs, chunk):
    rows = pl.ds(8 * chunk, 8)
    R = {t: rs[t, rows, 0:LANES] for t in range(16)}
    S = {t: rs[t, rows, LANES : 2 * LANES] for t in range(1, 16)}
    R[16] = rs[0, rows, LANES : 2 * LANES]
    return R, S


def leave_block(sources, metric, helm, table, waves, here, sent, source_here, metric_here, helm_here, arrived):
    moves = [(metric, metric_here)]
    moves += [(sources.at[f], source_here.at[f]) for f in range(2)] + [(helm, helm_here)]
    copies = [pltpu.make_async_copy(a, b, arrived.at[n]) for n, (a, b) in enumerate(moves)]
    for copy in copies:
        copy.start()
    copies[0].wait()
    inverse = 1.0 / metric_here[...]
    for f in range(2):
        copies[1 + f].wait()
        field = source_here[f] * inverse
        for h in range(2):
            across = field[LANES * h : LANES * (h + 1), :].T
            for quarter in range(4):
                rows = pl.ds(LANES * (4 * f + quarter) + h, BLOCK, stride=2)
                sent[rows, :] = across[BLOCK * quarter : BLOCK * (quarter + 1)]
    copies[3].wait()
    weight = helm_here[...] * (inverse * inverse) - SHIFT
    for h in range(2):
        across = weight[LANES * h : LANES * (h + 1), :].T
        for quarter in range(4):
            for f in range(2):
                rows = pl.ds(LANES * (4 * f + quarter) + 64 + h, BLOCK, stride=2)
                sent[rows, :] = across[BLOCK * quarter : BLOCK * (quarter + 1)]


def from_block(blocks, a, chunk, field):
    return blocks[pl.ds(LANES * (a // 2) + 64 * field + 16 * chunk + a % 2, 8, stride=2), :]


def lines(spectrum, y):
    return spectrum[pl.ds(16 * y, 16), :]


def forward_x(table, rs, spectrum):
    for t in range(16):
        spectrum[pl.ds(t, BLOCK, stride=16), :] = forward_dot(rs[t], table, t)


def backward_x(spectrum, table, rs):
    for t in range(16):
        rs[t] = backward_dot(spectrum[pl.ds(t, BLOCK, stride=16), :], table, t)


def leave_lines(spectrum, waves, here, ends, sent):
    rho, decay = waves[0], waves[1]
    p = lines(spectrum, 0)
    q = lines(spectrum, BLOCK - 1)
    for y in range(1, BLOCK):
        p = rho * p + lines(spectrum, y)
        q = rho * q + lines(spectrum, BLOCK - 1 - y)
    ends[0], ends[1] = p, q
    b = here[...]
    above = p + jnp.exp(-decay * (2.0 * b + 1.0)) * q
    below = q + jnp.exp(-decay * (2.0 * (BLOCKS - 1.0 - b) + 1.0)) * p
    for n in range(BLOCKS):
        sent[pl.ds(16 * n, 16), :] = jnp.where(b < n, above, below)


def solve_lines(received, spectrum, waves, here, ends, solved):
    rho, decay, scale, rounds = waves[0], waves[1], waves[2], waves[3]
    whole = jnp.exp(-decay)
    b = here[...]
    low = jnp.zeros((16, LANES), jnp.float32)
    high = jnp.zeros((16, LANES), jnp.float32)
    for n in range(BLOCKS):
        low = jnp.where(b > n, received[pl.ds(16 * n, 16), :] + whole * low, low)
        m = BLOCKS - 1 - n
        high = jnp.where(b < m, received[pl.ds(16 * m, 16), :] + whole * high, high)
    p, q = ends[0], ends[1]
    left = jnp.exp(-decay * (2.0 * b))
    right = jnp.exp(-decay * (2.0 * (BLOCKS - 1.0 - b)))
    up = (low + left * (q + whole * (high + right * p))) * rounds
    down = high + right * (p + whole * up)
    for y in range(BLOCK):
        up = rho * up + lines(spectrum, y)
        solved[pl.ds(16 * y, 16), :] = up
    for y in range(BLOCK - 1, -1, -1):
        down = rho * down
        solved[pl.ds(16 * y, 16), :] = scale * (lines(solved, y) + down)
        down = down + lines(spectrum, y)


def pencil_first(blocks, table, waves, here, sent, spectrum, ends, rs):
    for chunk in range(4):
        x = [from_block(blocks, a, chunk, 0) for a in range(16)]
        put_first(*first_stage(x), rs, chunk)
    forward_x(table, rs, spectrum)
    leave_lines(spectrum, waves, here, ends, sent)


def pencil_middle(received, blocks, old, old_ends, table, waves, here, sent, spectrum, ends, kept, rs, solved):
    solve_lines(received, old, waves, here, old_ends, solved)
    backward_x(solved, table, rs)
    for chunk in range(4):
        x = first_stage_transposed(*get_first(rs, chunk))
        for a in range(16):
            kept[a, pl.ds(8 * chunk, 8), :] = x[a]
        x = [x[a] * from_block(blocks, a, chunk, 1) for a in range(16)]
        put_first(*first_stage(x), rs, chunk)
    forward_x(table, rs, spectrum)
    leave_lines(spectrum, waves, here, ends, sent)


def pencil_last(received, blocks, old, old_ends, kept, table, waves, here, sent, rs, solved):
    solve_lines(received, old, waves, here, old_ends, solved)
    backward_x(solved, table, rs)
    sums = [jnp.zeros((8, LANES), jnp.float32) for _ in range(4)]
    for chunk in range(4):
        x = first_stage_transposed(*get_first(rs, chunk))
        for a in range(16):
            before, new = kept[a, pl.ds(8 * chunk, 8), :], x[a]
            weight = from_block(blocks, a, chunk, 1)
            scaled = weight * before
            sums[0] += from_block(blocks, a, chunk, 0) * before
            sums[1] += scaled * before
            sums[2] += scaled * new
            sums[3] += weight * new * new
            place = 136 * (a // 2) + 16 * chunk + a % 2
            sent[pl.ds(place, 8, stride=2), :] = before
            sent[pl.ds(place + 64, 8, stride=2), :] = new
    lane = lax.broadcasted_iota(jnp.int32, (8, LANES), 1)
    line = jnp.zeros((8, LANES), jnp.float32)
    for q in range(4):
        line = jnp.where(lane == q, jnp.sum(sums[q]), line)
    for i in range(8):
        sent[pl.ds(136 * i + 128, 8), :] = line


def gather_sums(received, sent):
    for f in range(2):
        total = received[pl.ds(136 * 4 * f + 128, 1), :]
        for quarter in range(1, 4):
            total += received[pl.ds(136 * (4 * f + quarter) + 128, 1), :]
        sent[pl.ds(f, 16, stride=2), :] = jnp.broadcast_to(total, (16, LANES))


def enter_block(received, parts, sources, metric, helm, solution, resid, near, done):
    copies = []
    lane = lax.broadcasted_iota(jnp.int32, (1, LANES), 1)
    m = metric[...]
    inverse = 1.0 / m
    weight = helm[...] * inverse - SHIFT * m
    for f in range(2):
        totals = jnp.sum(parts[pl.ds(f, 16, stride=2), :], axis=0, keepdims=True)
        n0, n1, n2, n3 = [
            jnp.sum(jnp.where(lane == q, totals, 0.0), axis=1, keepdims=True) for q in range(4)
        ]
        delta = n0 + n1
        alpha = n0 / delta
        rest = n1 / delta
        gamma = n0 * rest * rest - 2.0 * alpha * rest * n1 + alpha * alpha * n2
        beta = gamma / n0
        p, q = rest + beta, -alpha
        second = gamma / (p * p * delta + 2.0 * p * q * (n1 + n2) + q * q * (n2 + n3))
        c0, c1 = alpha + second * p, second * q
        for h in range(2):
            pair = []
            for field in range(2):
                places = [136 * (4 * f + quarter) + 64 * field + h for quarter in range(4)]
                columns = [received[pl.ds(place, BLOCK, stride=2), :] for place in places]
                pair.append(jnp.concatenate(columns, axis=0).T)
            old, new = pair
            rows = slice(LANES * h, LANES * (h + 1))
            near[0, f, rows, :] = (c0 * old + c1 * new) * inverse[rows]
            near[1, f, rows, :] = (1.0 - c0) * sources[f, rows, :] - ((c0 + c1) * old + c1 * new) * weight[rows]
            for n, out in enumerate((solution, resid)):
                place = (f, pl.ds(LANES * h, LANES))
                copies.append(pltpu.make_async_copy(near.at[n, *place], out.at[*place], done.at[4 * n + 2 * f + h]))
                copies[-1].start()
    for copy in copies:
        copy.wait()


RS = pltpu.VMEM((16, 32, 2 * LANES), jnp.float32)
LINES = pltpu.VMEM((512, LANES), jnp.float32)
SENT, SPECTRUM, ENDS, KEPT = (1024, LANES), (512, LANES), (2, 16, LANES), (16, 32, LANES)


def call(kernel, outs, scratch, **more):
    return pl.pallas_call(
        kernel,
        out_shape=[jax.ShapeDtypeStruct(s, jnp.float32) for s in outs],
        scratch_shapes=scratch,
        compiler_params=pltpu.CompilerParams(vmem_limit_bytes=32 * 1024 * 1024),
        **more,
    )


def far(*arrays):
    return [pltpu.with_memory_space_constraint(a, pltpu.HBM) for a in arrays]


def exchange(flat, axes, *shape):
    moved = lax.all_to_all(flat.reshape(*shape, LANES), axes, 0, 0, tiled=True)
    return moved.reshape(flat.shape)


def per_device(sources, metric, helm):
    table, waves = (jnp.asarray(a) for a in tables())
    line, column = ("half", "quarter"), ("gy", "quarter")
    here = lax.axis_index("gy") * lax.axis_size("quarter") + lax.axis_index("quarter")
    here = jnp.full((1, LANES), here, jnp.float32)
    block = pltpu.VMEM(metric.shape, metric.dtype)
    hbm, vmem = pl.BlockSpec(memory_space=pl.ANY), pl.BlockSpec(memory_space=pltpu.VMEM)

    (sent,) = call(
        leave_block,
        [SENT],
        [pltpu.VMEM(sources.shape, sources.dtype), block, block, pltpu.SemaphoreType.DMA((4,))],
        in_specs=[hbm] * 5 + [vmem],
    )(*far(sources, metric, helm, table, waves), here)
    blocks = exchange(sent, line, 8, 128)
    sent, first, ends = call(pencil_first, [SENT, SPECTRUM, ENDS], [RS])(blocks, table, waves, here)
    received = exchange(sent, column, BLOCKS, 16)
    sent, second, more, kept = call(pencil_middle, [SENT, SPECTRUM, ENDS, KEPT], [RS, LINES])(
        received, blocks, first, ends, table, waves, here
    )
    received = exchange(sent, column, BLOCKS, 16)
    (sent,) = call(pencil_last, [(8 * 136, LANES)], [RS, LINES])(
        received, blocks, second, more, kept, table, waves, here
    )
    received = exchange(sent, line, 8, 136)
    (parts,) = call(gather_sums, [(32, LANES)], [])(received)
    parts = exchange(parts, "gy", 16, 2)
    outs = call(
        enter_block,
        [sources.shape] * 2,
        [pltpu.VMEM((2, *sources.shape), jnp.float32), pltpu.SemaphoreType.DMA((8,))],
        in_specs=[vmem] * 5,
        out_specs=[hbm] * 2,
    )(received, parts, sources, metric, helm)
    return tuple(outs)


def solution(mesh):
    devices = mesh.devices.reshape(2, 4, 16)
    finer = jax.sharding.Mesh(devices, ("half", "quarter", "gy"))
    line = ("half", "quarter")
    in_specs = (P(None, line, "gy"), P(line, "gy"), P(line, "gy"))
    out_specs = (P(None, line, "gy"), P(None, line, "gy"))
    return jax.shard_map(
        per_device, mesh=finer, in_specs=in_specs, out_specs=out_specs, check_vma=False
    )
```

time: 106 us -> 83.9 us (0.79)
  blocking collectives: 95.2 us -> 77.1 us
  Pallas kernels: 7.91 us -> 5.71 us
  local copies, waits for them, and re-layouts: 1.8 us -> 0.03 us
    all_to_all x6 -> x5, blocking collectives: 95.2 us -> 77.1 us  [exchange(): moved = lax.all_to_all(flat.reshape(*shape, LANES), axes, 0, 0, tiled=True)]
    pallas_call x7 -> x6, Pallas kernels: 7.91 us -> 5.71 us  [the longest x1 1.51 us: per_device(): call(pencil_middle, [SENT, SPECTRUM, ENDS, KEPT], [RS, LINES])]
    unnamed x12 -> x10, local copies, waits for them, and re-layouts: 1.79 us -> 0.02 us
where the time goes in v2:
time: 83.9 us; the launch traced here: 83.6 us
  blocking collectives  77.1 us (92%)
  Pallas kernels  5.71 us (7%)
    all_to_all x5, blocking collectives, exchange(): moved = lax.all_to_all(flat.reshape(*shape, LANES), axes, 0, 0, tiled=True)  77.1 us

profile of v2, /device:TPU:0, one launch (start us, length us, event | category | flops | bytes accessed | tf_op | source)
XLA Modules:
  0.0 83.6 jit_solution(3779179956487507498)
XLA Ops:
  0.6 0.0 copy-start.2
  0.6 0.0 copy-start
  0.7 1.5 %shard_map.68 = f32[1024,128]{1,0:T(8,128)S(1)} custom-call(f32[2,256,128]{2,1,0:T(8,128)} %sources.3, f32[256,128]{1,0:T(8,128)} %metric.3, f32[256,128]{1,0:T(8,128)} %helm.3, bf16[16,2,256,256]{3,2,1,0:T(8,128)(2,1)} %constant.15.clone.table, f32[4,16,128]{2,1,0:T(8,128)} %constant.16.clone.waves, f32[1,128]{1,0:T(1,128)S(1)} %broadcast_in_dim.3.here), custom_call_target="tpu_custom_call" | custom-call | tf_op jit(solution)/shard_map/pallas_call | solution.py:353
  2.1 15.7 %all_to_all.25 = f32[8,128,128]{2,1,0:T(8,128)S(1)} all-to-all(f32[8,128,128]{2,1,0:T(8,128)S(1)} %bitcast.18), channel_id=1, replica_groups=mesh['half'=2,'quarter'=4,'gy'=16] {'half','quarter'}, dimensions={0} | all-to-all | bytes 1048576 | tf_op jit(solution)/shard_map/all_to_all | solution.py:341
  17.9 0.0 copy-done.2
  17.9 0.0 copy-done
  17.9 0.7 shard_map.69
  18.5 20.2 %all_to_all.26 = f32[64,16,128]{2,1,0:T(8,128)S(1)} all-to-all(f32[64,16,128]{2,1,0:T(8,128)S(1)} %bitcast.20), channel_id=1, replica_groups=mesh['half'=2,'quarter'=4,'gy'=16] {'gy','quarter'}, dimensions={0} | all-to-all | bytes 1048576 | tf_op jit(solution)/shard_map/all_to_all | solution.py:341
  38.8 1.5 %shard_map.70 = (f32[1024,128]{1,0:T(8,128)S(1)}, f32[512,128]{1,0:T(8,128)S(1)}, f32[2,16,128]{2,1,0:T(8,128)S(1)}, f32[16,32,128]{2,1,0:T(8,128)S(1)}) custom-call(f32[1024,128]{1,0:T(8,128)S(1)} %bitcast.17, f32[1024,128]{1,0:T(8,128)S(1)} %bitcast.11, f32[512,128]{1,0:T(8,128)S(1)} %get-tuple-element.10.old, ...), custom_call_target="tpu_custom_call" | custom-call | tf_op jit(solution)/shard_map/pallas_call | solution.py:362
  40.3 16.8 %all_to_all.27 = f32[64,16,128]{2,1,0:T(8,128)S(1)} all-to-all(f32[64,16,128]{2,1,0:T(8,128)S(1)} %bitcast.19), channel_id=1, replica_groups=mesh['half'=2,'quarter'=4,'gy'=16] {'gy','quarter'}, dimensions={0} | all-to-all | bytes 1048576 | tf_op jit(solution)/shard_map/all_to_all | solution.py:341
  57.1 0.0 copy-start.1
  57.1 0.0 copy-start.3
  57.1 0.0 copy-start.4
  57.1 1.1 %shard_map.71 = f32[1088,128]{1,0:T(8,128)S(1)} custom-call(f32[1024,128]{1,0:T(8,128)S(1)} %bitcast.16, f32[1024,128]{1,0:T(8,128)S(1)} %bitcast.12, f32[512,128]{1,0:T(8,128)S(1)} %get-tuple-element.13.old, f32[2,16,128]{2,1,0:T(8,128)S(1)} %get-tuple-element.14.old_ends, f32[16,32,128]{2,1,0:T(8,128)S(1)} %get-tuple-element.15.kept, ...), custom_call_target="tpu_custom_call" | custom-call | tf_op jit(solution)/shard_map/pallas_call | solution.py:366
  58.2 13.9 %all_to_all.28 = f32[8,136,128]{2,1,0:T(8,128)S(1)} all-to-all(f32[8,136,128]{2,1,0:T(8,128)S(1)} %bitcast.15), channel_id=1, replica_groups=mesh['half'=2,'quarter'=4,'gy'=16] {'half','quarter'}, dimensions={0} | all-to-all | bytes 1114112 | tf_op jit(solution)/shard_map/all_to_all | solution.py:341
  72.1 10.5 %all_to_all.29 = f32[16,2,128]{2,1,0:T(2,128)S(1)} all-to-all(f32[16,2,128]{2,1,0:T(2,128)S(1)} %bitcast.22), channel_id=1, replica_groups=mesh['half'=2,'quarter'=4,'gy'=16] {'gy'}, dimensions={0} | all-to-all | bytes 32768 | tf_op jit(solution)/shard_map/all_to_all | solution.py:341
  82.6 0.0 copy-done.1
  82.6 0.0 copy-done.3
  82.6 0.0 copy-done.4
  82.6 1.0 %shard_map.73 = (f32[2,256,128]{2,1,0:T(8,128)}, f32[2,256,128]{2,1,0:T(8,128)}) custom-call(f32[1088,128]{1,0:T(8,128)S(1)} %bitcast.14, f32[32,128]{1,0:T(8,128)S(1)} %bitcast.21, f32[2,256,128]{2,1,0:T(8,128)S(1)} %copy-done.1, f32[256,128]{1,0:T(8,128)S(1)} %copy-done.3, f32[256,128]{1,0:T(8,128)S(1)} %copy-done.4), custom_call_target="tpu_custom_call" | custom-call | tf_op jit(solution)/shard_map/pallas_call | solution.py:372
  (2 shorter events, 0.0 us)
Async XLA Ops:
  0.6 17.2 %copy-start.2 = (f32[4,16,128]{2,1,0:T(8,128)S(1)}, f32[4,16,128]{2,1,0:T(8,128)}, u32[]{:S(2)}) copy-start(f32[4,16,128]{2,1,0:T(8,128)} %constant.16.clone.waves) | copy-start | bytes 98308
  0.6 17.2 %copy-start = (bf16[16,2,256,256]{3,2,1,0:T(8,128)(2,1)S(1)}, bf16[16,2,256,256]{3,2,1,0:T(8,128)(2,1)}, u32[]{:S(2)}) copy-start(bf16[16,2,256,256]{3,2,1,0:T(8,128)(2,1)} %constant.15.clone.table) | copy-start | bytes 12582916
  57.1 25.5 %copy-start.1 = (f32[2,256,128]{2,1,0:T(8,128)S(1)}, f32[2,256,128]{2,1,0:T(8,128)}, u32[]{:S(2)}) copy-start(f32[2,256,128]{2,1,0:T(8,128)} %sources.3) | copy-start | bytes 786436
  57.1 25.5 %copy-start.3 = (f32[256,128]{1,0:T(8,128)S(1)}, f32[256,128]{1,0:T(8,128)}, u32[]{:S(2)}) copy-start(f32[256,128]{1,0:T(8,128)} %metric.3) | copy-start | bytes 393220
  57.1 25.5 %copy-start.4 = (f32[256,128]{1,0:T(8,128)S(1)}, f32[256,128]{1,0:T(8,128)}, u32[]{:S(2)}) copy-start(f32[256,128]{1,0:T(8,128)} %helm.3) | copy-start | bytes 393220

commit v3 on v2

--- a/solution.py
+++ b/solution.py
@@ -13,7 +13,7 @@
 SHIFT = 0.001
 ROWS = 16
 BLOCK = 32
-BLOCKS = 64
+BLOCKS = 32
 LANES = 128
 LENGTH = ROWS * LANES
 
@@ -43,7 +43,7 @@
     forward = np.concatenate([high, low], axis=2)
     sigma = 4.0 * np.sin(math.pi * freq / (2 * LENGTH)) ** 2 + SHIFT
     mu = 2.0 * np.arcsinh(np.sqrt(sigma) / 2.0)
-    waves = [np.exp(-mu), BLOCK * mu, 0.5 / np.sinh(mu), 1.0 / (1.0 - np.exp(-2.0 * BLOCK * BLOCKS * mu))]
+    waves = [np.exp(-mu), BLOCK * mu, 0.5 / np.sinh(mu), 1.0 / (1.0 - np.exp(-4.0 * BLOCK * BLOCKS * mu))]
     return np.stack([forward, np.swapaxes(forward, 1, 2)], axis=1), np.stack(waves).astype(np.float32)
 
 
@@ -144,7 +144,7 @@
     return R, S
 
 
-def leave_block(sources, metric, helm, table, waves, here, sent, source_here, metric_here, helm_here, arrived):
+def leave_block(sources, metric, helm, table, waves, here, core, sent, source_here, metric_here, helm_here, arrived):
     moves = [(metric, metric_here)]
     moves += [(sources.at[f], source_here.at[f]) for f in range(2)] + [(helm, helm_here)]
     copies = [pltpu.make_async_copy(a, b, arrived.at[n]) for n, (a, b) in enumerate(moves)]
@@ -188,36 +188,55 @@
         rs[t] = backward_dot(spectrum[pl.ds(t, BLOCK, stride=16), :], table, t)
 
 
-def leave_lines(spectrum, waves, here, ends, sent):
-    rho, decay = waves[0], waves[1]
+def local_sums(spectrum, waves, ends):
+    rho = waves[0]
     p = lines(spectrum, 0)
     q = lines(spectrum, BLOCK - 1)
     for y in range(1, BLOCK):
         p = rho * p + lines(spectrum, y)
         q = rho * q + lines(spectrum, BLOCK - 1 - y)
     ends[0], ends[1] = p, q
+
+
+def both_cores(ends, sibling, whole, upper):
+    p = jnp.where(upper, ends[0] + whole * sibling[0], sibling[0] + whole * ends[0])
+    q = jnp.where(upper, sibling[1] + whole * ends[1], ends[1] + whole * sibling[1])
+    return p, q
+
+
+def leave_lines(ends, sibling, waves, here, core, sent):
+    decay = waves[1]
+    upper = core[...] > 0
+    p, q = both_cores(ends, sibling, jnp.exp(-decay), upper)
     b = here[...]
-    above = p + jnp.exp(-decay * (2.0 * b + 1.0)) * q
-    below = q + jnp.exp(-decay * (2.0 * (BLOCKS - 1.0 - b) + 1.0)) * p
+    above = p + jnp.exp(-decay * (4.0 * b + 2.0)) * q
+    below = q + jnp.exp(-decay * (4.0 * (BLOCKS - 1.0 - b) + 2.0)) * p
+    above = jnp.where(upper, above[8:], above[:8])
+    below = jnp.where(upper, below[8:], below[:8])
     for n in range(BLOCKS):
-        sent[pl.ds(16 * n, 16), :] = jnp.where(b < n, above, below)
-
-
-def solve_lines(received, spectrum, waves, here, ends, solved):
+        value = jnp.where(b < n, above, below)
+        for twin in range(2):
+            sent[pl.ds(16 * n + 8 * twin, 8), :] = value
+
+
+def solve_lines(received, spectrum, waves, here, core, ends, sibling, solved):
     rho, decay, scale, rounds = waves[0], waves[1], waves[2], waves[3]
-    whole = jnp.exp(-decay)
+    whole, double = jnp.exp(-decay), jnp.exp(-2.0 * decay)
     b = here[...]
     low = jnp.zeros((16, LANES), jnp.float32)
     high = jnp.zeros((16, LANES), jnp.float32)
     for n in range(BLOCKS):
-        low = jnp.where(b > n, received[pl.ds(16 * n, 16), :] + whole * low, low)
+        low = jnp.where(b > n, received[pl.ds(16 * n, 16), :] + double * low, low)
         m = BLOCKS - 1 - n
-        high = jnp.where(b < m, received[pl.ds(16 * m, 16), :] + whole * high, high)
-    p, q = ends[0], ends[1]
-    left = jnp.exp(-decay * (2.0 * b))
-    right = jnp.exp(-decay * (2.0 * (BLOCKS - 1.0 - b)))
-    up = (low + left * (q + whole * (high + right * p))) * rounds
-    down = high + right * (p + whole * up)
+        high = jnp.where(b < m, received[pl.ds(16 * m, 16), :] + double * high, high)
+    upper = core[...] > 0
+    p, q = both_cores(ends, sibling, whole, upper)
+    left = jnp.exp(-decay * (4.0 * b))
+    right = jnp.exp(-decay * (4.0 * (BLOCKS - 1.0 - b)))
+    up = (low + left * (q + double * (high + right * p))) * rounds
+    down = high + right * (p + double * up)
+    up = jnp.where(upper, sibling[0] + whole * up, up)
+    down = jnp.where(upper, down, sibling[1] + whole * down)
     for y in range(BLOCK):
         up = rho * up + lines(spectrum, y)
         solved[pl.ds(16 * y, 16), :] = up
@@ -227,16 +246,18 @@
         down = down + lines(spectrum, y)
 
 
-def pencil_first(blocks, table, waves, here, sent, spectrum, ends, rs):
+def pencil_first(blocks, table, waves, spectrum, ends, rs):
     for chunk in range(4):
         x = [from_block(blocks, a, chunk, 0) for a in range(16)]
         put_first(*first_stage(x), rs, chunk)
     forward_x(table, rs, spectrum)
-    leave_lines(spectrum, waves, here, ends, sent)
-
-
-def pencil_middle(received, blocks, old, old_ends, table, waves, here, sent, spectrum, ends, kept, rs, solved):
-    solve_lines(received, old, waves, here, old_ends, solved)
+    local_sums(spectrum, waves, ends)
+
+
+def pencil_middle(
+    received, blocks, old, old_ends, sibling, table, waves, here, core, spectrum, ends, kept, rs, solved
+):
+    solve_lines(received, old, waves, here, core, old_ends, sibling, solved)
     backward_x(solved, table, rs)
     for chunk in range(4):
         x = first_stage_transposed(*get_first(rs, chunk))
@@ -245,11 +266,11 @@
         x = [x[a] * from_block(blocks, a, chunk, 1) for a in range(16)]
         put_first(*first_stage(x), rs, chunk)
     forward_x(table, rs, spectrum)
-    leave_lines(spectrum, waves, here, ends, sent)
-
-
-def pencil_last(received, blocks, old, old_ends, kept, table, waves, here, sent, rs, solved):
-    solve_lines(received, old, waves, here, old_ends, solved)
+    local_sums(spectrum, waves, ends)
+
+
+def pencil_last(received, blocks, old, old_ends, sibling, kept, table, waves, here, core, sent, rs, solved):
+    solve_lines(received, old, waves, here, core, old_ends, sibling, solved)
     backward_x(solved, table, rs)
     sums = [jnp.zeros((8, LANES), jnp.float32) for _ in range(4)]
     for chunk in range(4):
@@ -320,7 +341,8 @@
 
 RS = pltpu.VMEM((16, 32, 2 * LANES), jnp.float32)
 LINES = pltpu.VMEM((512, LANES), jnp.float32)
-SENT, SPECTRUM, ENDS, KEPT = (1024, LANES), (512, LANES), (2, 16, LANES), (16, 32, LANES)
+BLOCKS_SENT, SENT, SPECTRUM = (1024, LANES), (512, LANES), (512, LANES)
+ENDS, KEPT = (2, 16, LANES), (16, 32, LANES)
 
 
 def call(kernel, outs, scratch, **more):
@@ -344,27 +366,35 @@
 
 def per_device(sources, metric, helm):
     table, waves = (jnp.asarray(a) for a in tables())
-    line, column = ("half", "quarter"), ("gy", "quarter")
-    here = lax.axis_index("gy") * lax.axis_size("quarter") + lax.axis_index("quarter")
+    line, column = ("half", "pair", "core"), ("gy", "pair", "core")
+    here = lax.axis_index("gy") * lax.axis_size("pair") + lax.axis_index("pair")
     here = jnp.full((1, LANES), here, jnp.float32)
+    core = jnp.full((1, LANES), lax.axis_index("core"), jnp.float32)
     block = pltpu.VMEM(metric.shape, metric.dtype)
     hbm, vmem = pl.BlockSpec(memory_space=pl.ANY), pl.BlockSpec(memory_space=pltpu.VMEM)
 
+    def swap(ends):
+        return lax.ppermute(ends, "core", [(0, 1), (1, 0)])
+
     (sent,) = call(
         leave_block,
-        [SENT],
+        [BLOCKS_SENT],
         [pltpu.VMEM(sources.shape, sources.dtype), block, block, pltpu.SemaphoreType.DMA((4,))],
-        in_specs=[hbm] * 5 + [vmem],
-    )(*far(sources, metric, helm, table, waves), here)
+        in_specs=[hbm] * 5 + [vmem] * 2,
+    )(*far(sources, metric, helm, table, waves), here, core)
     blocks = exchange(sent, line, 8, 128)
-    sent, first, ends = call(pencil_first, [SENT, SPECTRUM, ENDS], [RS])(blocks, table, waves, here)
-    received = exchange(sent, column, BLOCKS, 16)
-    sent, second, more, kept = call(pencil_middle, [SENT, SPECTRUM, ENDS, KEPT], [RS, LINES])(
-        received, blocks, first, ends, table, waves, here
+    first, ends = call(pencil_first, [SPECTRUM, ENDS], [RS])(blocks, table, waves)
+    sibling = swap(ends)
+    (sent,) = call(leave_lines, [SENT], [])(ends, sibling, waves, here, core)
+    received = exchange(sent, column, 64, 8)
+    second, more, kept = call(pencil_middle, [SPECTRUM, ENDS, KEPT], [RS, LINES])(
+        received, blocks, first, ends, sibling, table, waves, here, core
     )
-    received = exchange(sent, column, BLOCKS, 16)
+    twin = swap(more)
+    (sent,) = call(leave_lines, [SENT], [])(more, twin, waves, here, core)
+    received = exchange(sent, column, 64, 8)
     (sent,) = call(pencil_last, [(8 * 136, LANES)], [RS, LINES])(
-        received, blocks, second, more, kept, table, waves, here
+        received, blocks, second, more, twin, kept, table, waves, here, core
     )
     received = exchange(sent, line, 8, 136)
     (parts,) = call(gather_sums, [(32, LANES)], [])(received)
@@ -380,9 +410,9 @@
 
 
 def solution(mesh):
-    devices = mesh.devices.reshape(2, 4, 16)
-    finer = jax.sharding.Mesh(devices, ("half", "quarter", "gy"))
-    line = ("half", "quarter")
+    devices = mesh.devices.reshape(2, 2, 2, 16)
+    finer = jax.sharding.Mesh(devices, ("half", "pair", "core", "gy"))
+    line = ("half", "pair", "core")
     in_specs = (P(None, line, "gy"), P(line, "gy"), P(line, "gy"))
     out_specs = (P(None, line, "gy"), P(None, line, "gy"))
     return jax.shard_map(

time: 83.9 us -> 81 us (0.965)
  blocking collectives: 77.1 us -> 72 us
  waiting for transfers between devices: 0 us -> 2.27 us
    all_to_all x5, blocking collectives: 77.1 us -> 72 us  [exchange(): moved = lax.all_to_all(flat.reshape(*shape, LANES), axes, 0, 0, tiled=True)]
    ppermute x0 -> x2, waiting for transfers between devices: none -> 2.27 us  [swap(): return lax.ppermute(ends, 'core', [(0, 1), (1, 0)])]
    pallas_call x3 -> x5, Pallas kernels: 3.64 us -> 3.48 us  [the longest x1 1.46 us: per_device(): call(leave_block, [BLOCKS_SENT], [pltpu.VMEM(sources.shape, sources.dtype...]
  transfers between devices with their start and end apart: 0 -> 2, of which waited for: 0 -> 2; matrix products, arithmetic and copies ran while one was open for 0% -> 0% of each run, Pallas kernels for 0% -> 0%
where the time goes in v3:
time: 81 us; the launch traced here: 80.7 us
  blocking collectives  72 us (89%)
  Pallas kernels  5.44 us (7%)
  waiting for transfers between devices  2.27 us (3%)
    all_to_all x5, blocking collectives, exchange(): moved = lax.all_to_all(flat.reshape(*shape, LANES), axes, 0, 0, tiled=True)  72 us
    ppermute x2, waiting for transfers between devices, swap(): return lax.ppermute(ends, 'core', [(0, 1), (1, 0)])  2.27 us
  transfers between devices with their start and end apart: 2, of which 2 were waited for; matrix products, arithmetic and copies ran while one was open for 0% of the time, Pallas kernels for 0%

profile of v3, /device:TPU:0, one launch (start us, length us, event | category | flops | bytes accessed | tf_op | source)
XLA Modules:
  0.0 80.7 jit_solution(7148023600919324517)
XLA Ops:
  0.6 0.0 copy-start.1
  0.7 0.0 copy-start
  0.7 1.5 %shard_map.68 = f32[1024,128]{1,0:T(8,128)S(1)} custom-call(f32[2,256,128]{2,1,0:T(8,128)} %sources.3, f32[256,128]{1,0:T(8,128)} %metric.3, f32[256,128]{1,0:T(8,128)} %helm.3, bf16[16,2,256,256]{3,2,1,0:T(8,128)(2,1)} %constant.19.clone.table, f32[4,16,128]{2,1,0:T(8,128)} %constant.20.clone.waves, f32[1,128]{1,0:T(1,128)S(1)} %broadcast_in_dim.6.here, ...), custom_call_target="tpu_custom_call" | custom-call | tf_op jit(solution)/shard_map/pallas_call | solution.py:379
  2.2 15.6 %all_to_all.25 = f32[8,128,128]{2,1,0:T(8,128)S(1)} all-to-all(f32[8,128,128]{2,1,0:T(8,128)S(1)} %bitcast.16), channel_id=1, replica_groups=mesh['half'=2,'pair'=2,'core'=2,'gy'=16] {'half','pair','core'}, dimensions={0} | all-to-all | bytes 1048576 | tf_op jit(solution)/shard_map/all_to_all | solution.py:363
  17.7 0.0 copy-done.1
  17.8 0.0 copy-done
  17.8 0.6 shard_map.69
  18.4 0.1 collective-permute-start
  18.4 1.2 %collective-permute-done.sibling = f32[2,16,128]{2,1,0:T(8,128)S(1)} collective-permute-done((f32[2,16,128]{2,1,0:T(8,128)S(1)}, f32[2,16,128]{2,1,0:T(8,128)S(1)}, u32[]{:S(2)}, u32[]{:S(2)}) %collective-permute-start) | collective-permute-done | bytes 16416 | tf_op jit(solution)/shard_map/ppermute | solution.py:377
  19.7 17.5 %all_to_all.26 = f32[64,8,128]{2,1,0:T(8,128)S(1)} all-to-all(f32[64,8,128]{2,1,0:T(8,128)S(1)} %bitcast.19), channel_id=1, replica_groups=mesh['half'=2,'pair'=2,'core'=2,'gy'=16] {'gy','pair','core'}, dimensions={0} | all-to-all | bytes 524288 | tf_op jit(solution)/shard_map/all_to_all | solution.py:363
  37.2 1.3 %shard_map.71 = (f32[512,128]{1,0:T(8,128)S(1)}, f32[2,16,128]{2,1,0:T(8,128)S(1)}, f32[16,32,128]{2,1,0:T(8,128)S(1)}) custom-call(f32[512,128]{1,0:T(8,128)S(1)} %bitcast.18, f32[1024,128]{1,0:T(8,128)S(1)} %bitcast.11, f32[512,128]{1,0:T(8,128)S(1)} %get-tuple-element.8.old, f32[2,16,128]{2,1,0:T(8,128)S(1)} %get-tuple-element.7.ends.old_ends, ...), custom_call_target="tpu_custom_call" | custom-call | tf_op jit(solution)/shard_map/pallas_call | solution.py:390
  38.5 0.2 collective-permute-start.1
  38.7 1.1 %collective-permute-done.1.sibling = f32[2,16,128]{2,1,0:T(8,128)S(1)} collective-permute-done((f32[2,16,128]{2,1,0:T(8,128)S(1)}, f32[2,16,128]{2,1,0:T(8,128)S(1)}, u32[]{:S(2)}, u32[]{:S(2)}) %collective-permute-start.1) | collective-permute-done | bytes 16416 | tf_op jit(solution)/shard_map/ppermute | solution.py:377
  39.8 0.0 copy-start.2
  39.8 0.0 copy-start.3
  39.9 0.0 copy-start.4
  39.9 14.2 %all_to_all.27 = f32[64,8,128]{2,1,0:T(8,128)S(1)} all-to-all(f32[64,8,128]{2,1,0:T(8,128)S(1)} %bitcast.20), channel_id=1, replica_groups=mesh['half'=2,'pair'=2,'core'=2,'gy'=16] {'gy','pair','core'}, dimensions={0} | all-to-all | bytes 524288 | tf_op jit(solution)/shard_map/all_to_all | solution.py:363
  54.1 0.9 %shard_map.73 = f32[1088,128]{1,0:T(8,128)S(1)} custom-call(f32[512,128]{1,0:T(8,128)S(1)} %bitcast.17, f32[1024,128]{1,0:T(8,128)S(1)} %bitcast.12, f32[512,128]{1,0:T(8,128)S(1)} %get-tuple-element.10.old, f32[2,16,128]{2,1,0:T(8,128)S(1)} %get-tuple-element.9.ends.old_ends, f32[2,16,128]{2,1,0:T(8,128)S(1)} %collective-permute-done.1.sibling, ...), custom_call_target="tpu_custom_call" | custom-call | tf_op jit(solution)/shard_map/pallas_call | solution.py:396
  55.1 13.9 %all_to_all.28 = f32[8,136,128]{2,1,0:T(8,128)S(1)} all-to-all(f32[8,136,128]{2,1,0:T(8,128)S(1)} %bitcast.15), channel_id=1, replica_groups=mesh['half'=2,'pair'=2,'core'=2,'gy'=16] {'half','pair','core'}, dimensions={0} | all-to-all | bytes 1114112 | tf_op jit(solution)/shard_map/all_to_all | solution.py:363
  69.0 10.8 %all_to_all.29 = f32[16,2,128]{2,1,0:T(2,128)S(1)} all-to-all(f32[16,2,128]{2,1,0:T(2,128)S(1)} %bitcast.22), channel_id=1, replica_groups=mesh['half'=2,'pair'=2,'core'=2,'gy'=16] {'gy'}, dimensions={0} | all-to-all | bytes 32768 | tf_op jit(solution)/shard_map/all_to_all | solution.py:363
  79.7 0.0 copy-done.2
  79.7 0.0 copy-done.3
  79.7 0.0 copy-done.4
  79.7 1.0 %shard_map.75 = (f32[2,256,128]{2,1,0:T(8,128)}, f32[2,256,128]{2,1,0:T(8,128)}) custom-call(f32[1088,128]{1,0:T(8,128)S(1)} %bitcast.14, f32[32,128]{1,0:T(8,128)S(1)} %bitcast.21, f32[2,256,128]{2,1,0:T(8,128)S(1)} %copy-done.2, f32[256,128]{1,0:T(8,128)S(1)} %copy-done.3, f32[256,128]{1,0:T(8,128)S(1)} %copy-done.4), custom_call_target="tpu_custom_call" | custom-call | tf_op jit(solution)/shard_map/pallas_call | solution.py:402
  (5 shorter events, 0.1 us)
Async XLA Ops:
  0.6 17.1 %copy-start.1 = (f32[4,16,128]{2,1,0:T(8,128)S(1)}, f32[4,16,128]{2,1,0:T(8,128)}, u32[]{:S(2)}) copy-start(f32[4,16,128]{2,1,0:T(8,128)} %constant.20.clone.waves) | copy-start | bytes 98308
  0.7 17.1 %copy-start = (bf16[16,2,256,256]{3,2,1,0:T(8,128)(2,1)S(1)}, bf16[16,2,256,256]{3,2,1,0:T(8,128)(2,1)}, u32[]{:S(2)}) copy-start(bf16[16,2,256,256]{3,2,1,0:T(8,128)(2,1)} %constant.19.clone.table) | copy-start | bytes 12582916
  18.4 1.3 %collective-permute-start = (f32[2,16,128]{2,1,0:T(8,128)S(1)}, f32[2,16,128]{2,1,0:T(8,128)S(1)}, u32[]{:S(2)}, u32[]{:S(2)}) collective-permute-start(f32[2,16,128]{2,1,0:T(8,128)S(1)} %get-tuple-element.7.ends.old_ends), channel_id=1, source_target_pairs={{0,16},{16,0},{1,17},{17,1},{2,18},{18,2},{3,19},{19,3},{4,20},{20... | collective-permute-start | bytes 49160 | tf_op jit(solution)/shard_map/ppermute | solution.py:377
  38.5 1.3 %collective-permute-start.1 = (f32[2,16,128]{2,1,0:T(8,128)S(1)}, f32[2,16,128]{2,1,0:T(8,128)S(1)}, u32[]{:S(2)}, u32[]{:S(2)}) collective-permute-start(f32[2,16,128]{2,1,0:T(8,128)S(1)} %get-tuple-element.9.ends.old_ends), channel_id=1, source_target_pairs={{0,16},{16,0},{1,17},{17,1},{2,18},{18,2},{3,19},{19,3},{4,20},{20... | collective-permute-start | bytes 49160 | tf_op jit(solution)/shard_map/ppermute | solution.py:377
  39.8 39.9 %copy-start.2 = (f32[2,256,128]{2,1,0:T(8,128)S(1)}, f32[2,256,128]{2,1,0:T(8,128)}, u32[]{:S(2)}) copy-start(f32[2,256,128]{2,1,0:T(8,128)} %sources.3) | copy-start | bytes 786436
  39.8 39.9 %copy-start.3 = (f32[256,128]{1,0:T(8,128)S(1)}, f32[256,128]{1,0:T(8,128)}, u32[]{:S(2)}) copy-start(f32[256,128]{1,0:T(8,128)} %metric.3) | copy-start | bytes 393220
  39.9 39.9 %copy-start.4 = (f32[256,128]{1,0:T(8,128)S(1)}, f32[256,128]{1,0:T(8,128)}, u32[]{:S(2)}) copy-start(f32[256,128]{1,0:T(8,128)} %helm.3) | copy-start | bytes 393220

commit v4 on v3

--- a/solution.py
+++ b/solution.py
@@ -255,72 +255,91 @@
 
 
 def pencil_middle(
-    received, blocks, old, old_ends, sibling, table, waves, here, core, spectrum, ends, kept, rs, solved
+    received, blocks, old, old_ends, sibling, table, waves, here, core, spectrum, ends, kept, sums, rs, solved
 ):
     solve_lines(received, old, waves, here, core, old_ends, sibling, solved)
     backward_x(solved, table, rs)
+    totals = [jnp.zeros((8, LANES), jnp.float32) for _ in range(2)]
     for chunk in range(4):
         x = first_stage_transposed(*get_first(rs, chunk))
+        scaled = [x[a] * from_block(blocks, a, chunk, 1) for a in range(16)]
         for a in range(16):
             kept[a, pl.ds(8 * chunk, 8), :] = x[a]
-        x = [x[a] * from_block(blocks, a, chunk, 1) for a in range(16)]
-        put_first(*first_stage(x), rs, chunk)
+            totals[0] += from_block(blocks, a, chunk, 0) * x[a]
+            totals[1] += scaled[a] * x[a]
+        put_first(*first_stage(scaled), rs, chunk)
+    sums[0], sums[1] = totals
     forward_x(table, rs, spectrum)
     local_sums(spectrum, waves, ends)
 
 
-def pencil_last(received, blocks, old, old_ends, sibling, kept, table, waves, here, core, sent, rs, solved):
+def pencil_last(received, blocks, old, old_ends, sibling, kept, first, table, waves, here, core, sent, rs, solved):
     solve_lines(received, old, waves, here, core, old_ends, sibling, solved)
     backward_x(solved, table, rs)
-    sums = [jnp.zeros((8, LANES), jnp.float32) for _ in range(4)]
+    n0, n1 = (jnp.sum(first[n], axis=(0, 1), keepdims=True) for n in range(2))
+    positive = n0 + n1 > 0.0
+    step = jnp.where(positive, n0 / jnp.where(positive, n0 + n1, 1.0), 0.0)
+    step = jnp.clip(step, 0.0, 2.0)
+    sums = [jnp.zeros((8, LANES), jnp.float32) for _ in range(7)]
     for chunk in range(4):
         x = first_stage_transposed(*get_first(rs, chunk))
         for a in range(16):
             before, new = kept[a, pl.ds(8 * chunk, 8), :], x[a]
-            weight = from_block(blocks, a, chunk, 1)
-            scaled = weight * before
-            sums[0] += from_block(blocks, a, chunk, 0) * before
-            sums[1] += scaled * before
-            sums[2] += scaled * new
-            sums[3] += weight * new * new
+            weight, source = from_block(blocks, a, chunk, 1), from_block(blocks, a, chunk, 0)
+            g, h = source + weight * before, before + new
+            u1, z1 = source - step * g, before - step * h
+            wz, wh = weight * z1, weight * h
+            for q, (one, two) in enumerate(((u1, z1), (u1, h), (g, z1), (g, h), (wz, z1), (wz, h), (wh, h))):
+                sums[q] += one * two
             place = 136 * (a // 2) + 16 * chunk + a % 2
             sent[pl.ds(place, 8, stride=2), :] = before
             sent[pl.ds(place + 64, 8, stride=2), :] = new
     lane = lax.broadcasted_iota(jnp.int32, (8, LANES), 1)
-    line = jnp.zeros((8, LANES), jnp.float32)
-    for q in range(4):
-        line = jnp.where(lane == q, jnp.sum(sums[q]), line)
+    line = jnp.where(lane == 7, n0, jnp.where(lane == 8, n1, jnp.where(lane == 9, step, 0.0)))
+    for q in range(7):
+        line = jnp.where(lane == q, jnp.sum(sums[q], axis=(0, 1), keepdims=True), line)
     for i in range(8):
         sent[pl.ds(136 * i + 128, 8), :] = line
 
 
 def gather_sums(received, sent):
-    for f in range(2):
-        total = received[pl.ds(136 * 4 * f + 128, 1), :]
-        for quarter in range(1, 4):
-            total += received[pl.ds(136 * (4 * f + quarter) + 128, 1), :]
-        sent[pl.ds(f, 16, stride=2), :] = jnp.broadcast_to(total, (16, LANES))
+    row = lax.broadcasted_iota(jnp.int32, (8, LANES), 0)
+    rows = received[pl.ds(128, 8), :]
+    for i in range(1, 8):
+        rows = jnp.where(row == i, received[pl.ds(136 * i + 128, 8), :], rows)
+    for n in range(16):
+        sent[pl.ds(8 * n, 8), :] = rows
 
 
 def enter_block(received, parts, sources, metric, helm, solution, resid, near, done):
     copies = []
     lane = lax.broadcasted_iota(jnp.int32, (1, LANES), 1)
+    row = lax.broadcasted_iota(jnp.int32, (LANES, LANES), 0)
+    every = parts[...]
+    steps = jnp.sum(jnp.where(lane == 9, every, 0.0), axis=1, keepdims=True)
+
+    def pick(line, q):
+        return jnp.sum(jnp.where(lane == q, line, 0.0), axis=1, keepdims=True)
+
     m = metric[...]
     inverse = 1.0 / m
     weight = helm[...] * inverse - SHIFT * m
     for f in range(2):
-        totals = jnp.sum(parts[pl.ds(f, 16, stride=2), :], axis=0, keepdims=True)
-        n0, n1, n2, n3 = [
-            jnp.sum(jnp.where(lane == q, totals, 0.0), axis=1, keepdims=True) for q in range(4)
-        ]
+        mine = jnp.where(row % 8 // 4 == f, every, 0.0)
+        zeroth = jnp.sum(mine, axis=0, keepdims=True)
+        n0, n1 = pick(zeroth, 7), pick(zeroth, 8)
         delta = n0 + n1
-        alpha = n0 / delta
-        rest = n1 / delta
-        gamma = n0 * rest * rest - 2.0 * alpha * rest * n1 + alpha * alpha * n2
+        alpha, rest = n0 / delta, n1 / delta
+        away = alpha - steps
+        moved = away * mine
+        first = jnp.sum(moved, axis=0, keepdims=True)
+        second = jnp.sum(away * moved, axis=0, keepdims=True)
+        gamma = pick(zeroth, 0) - (pick(first, 1) + pick(first, 2)) + pick(second, 3)
+        inner = pick(zeroth, 4) - 2.0 * pick(first, 5) + pick(second, 6)
+        cross = pick(zeroth, 2) - pick(first, 3)
         beta = gamma / n0
-        p, q = rest + beta, -alpha
-        second = gamma / (p * p * delta + 2.0 * p * q * (n1 + n2) + q * q * (n2 + n3))
-        c0, c1 = alpha + second * p, second * q
+        size = gamma / (gamma + inner + 2.0 * beta * cross + beta * beta * delta)
+        c0, c1 = alpha + size * (rest + beta), -size * alpha
         for h in range(2):
             pair = []
             for field in range(2):
@@ -387,18 +406,18 @@
     sibling = swap(ends)
     (sent,) = call(leave_lines, [SENT], [])(ends, sibling, waves, here, core)
     received = exchange(sent, column, 64, 8)
-    second, more, kept = call(pencil_middle, [SPECTRUM, ENDS, KEPT], [RS, LINES])(
+    second, more, kept, sums = call(pencil_middle, [SPECTRUM, ENDS, KEPT, (2, 8, LANES)], [RS, LINES])(
         received, blocks, first, ends, sibling, table, waves, here, core
     )
     twin = swap(more)
     (sent,) = call(leave_lines, [SENT], [])(more, twin, waves, here, core)
     received = exchange(sent, column, 64, 8)
     (sent,) = call(pencil_last, [(8 * 136, LANES)], [RS, LINES])(
-        received, blocks, second, more, twin, kept, table, waves, here, core
+        received, blocks, second, more, twin, kept, sums, table, waves, here, core
     )
     received = exchange(sent, line, 8, 136)
-    (parts,) = call(gather_sums, [(32, LANES)], [])(received)
-    parts = exchange(parts, "gy", 16, 2)
+    (parts,) = call(gather_sums, [(LANES, LANES)], [])(received)
+    parts = exchange(parts, "gy", 16, 8)
     outs = call(
         enter_block,
         [sources.shape] * 2,

time: 81 us -> 81.4 us (level)
  no operation moved by 1% of the time
where the time goes in v4:
time: 81.4 us; the launch traced here: 81.1 us
  blocking collectives  72.1 us (89%)
  Pallas kernels  5.7 us (7%)
  waiting for transfers between devices  2.27 us (3%)
    all_to_all x5, blocking collectives, exchange(): moved = lax.all_to_all(flat.reshape(*shape, LANES), axes, 0, 0, tiled=True)  72.1 us
    ppermute x2, waiting for transfers between devices, swap(): return lax.ppermute(ends, 'core', [(0, 1), (1, 0)])  2.27 us
  transfers between devices with their start and end apart: 2, of which 2 were waited for; matrix products, arithmetic and copies ran while one was open for 0% of the time, Pallas kernels for 0%

profile of v4, /device:TPU:0, one launch (start us, length us, event | category | flops | bytes accessed | tf_op | source)
XLA Modules:
  0.0 81.1 jit_solution(13309979014000583737)
XLA Ops:
  0.6 0.0 copy-start.1
  0.7 0.0 copy-start
  0.7 1.5 %shard_map.68 = f32[1024,128]{1,0:T(8,128)S(1)} custom-call(f32[2,256,128]{2,1,0:T(8,128)} %sources.3, f32[256,128]{1,0:T(8,128)} %metric.3, f32[256,128]{1,0:T(8,128)} %helm.3, bf16[16,2,256,256]{3,2,1,0:T(8,128)(2,1)} %constant.19.clone.table, f32[4,16,128]{2,1,0:T(8,128)} %constant.20.clone.waves, f32[1,128]{1,0:T(1,128)S(1)} %broadcast_in_dim.6.here, ...), custom_call_target="tpu_custom_call" | custom-call | tf_op jit(solution)/shard_map/pallas_call | solution.py:398
  2.2 15.6 %all_to_all.25 = f32[8,128,128]{2,1,0:T(8,128)S(1)} all-to-all(f32[8,128,128]{2,1,0:T(8,128)S(1)} %bitcast.16), channel_id=1, replica_groups=mesh['half'=2,'pair'=2,'core'=2,'gy'=16] {'half','pair','core'}, dimensions={0} | all-to-all | bytes 1048576 | tf_op jit(solution)/shard_map/all_to_all | solution.py:382
  17.7 0.0 copy-done.1
  17.8 0.0 copy-done
  17.8 0.6 shard_map.69
  18.3 0.1 collective-permute-start
  18.4 1.2 %collective-permute-done.sibling = f32[2,16,128]{2,1,0:T(8,128)S(1)} collective-permute-done((f32[2,16,128]{2,1,0:T(8,128)S(1)}, f32[2,16,128]{2,1,0:T(8,128)S(1)}, u32[]{:S(2)}, u32[]{:S(2)}) %collective-permute-start) | collective-permute-done | bytes 16416 | tf_op jit(solution)/shard_map/ppermute | solution.py:396
  19.6 17.5 %all_to_all.26 = f32[64,8,128]{2,1,0:T(8,128)S(1)} all-to-all(f32[64,8,128]{2,1,0:T(8,128)S(1)} %bitcast.19), channel_id=1, replica_groups=mesh['half'=2,'pair'=2,'core'=2,'gy'=16] {'gy','pair','core'}, dimensions={0} | all-to-all | bytes 524288 | tf_op jit(solution)/shard_map/all_to_all | solution.py:382
  37.2 1.3 %shard_map.71 = (f32[512,128]{1,0:T(8,128)S(1)}, f32[2,16,128]{2,1,0:T(8,128)S(1)}, f32[16,32,128]{2,1,0:T(8,128)S(1)}, f32[2,8,128]{2,1,0:T(8,128)S(1)}) custom-call(f32[512,128]{1,0:T(8,128)S(1)} %bitcast.18, f32[1024,128]{1,0:T(8,128)S(1)} %bitcast.11, f32[512,128]{1,0:T(8,128)S(1)} %get-tuple-element.9.old, ...), custom_call_target="tpu_custom_call" | custom-call | tf_op jit(solution)/shard_map/pallas_call | solution.py:409
  38.5 0.2 collective-permute-start.1
  38.7 1.1 %collective-permute-done.1.sibling = f32[2,16,128]{2,1,0:T(8,128)S(1)} collective-permute-done((f32[2,16,128]{2,1,0:T(8,128)S(1)}, f32[2,16,128]{2,1,0:T(8,128)S(1)}, u32[]{:S(2)}, u32[]{:S(2)}) %collective-permute-start.1) | collective-permute-done | bytes 16416 | tf_op jit(solution)/shard_map/ppermute | solution.py:396
  39.8 0.0 copy-start.2
  39.8 0.0 copy-start.3
  39.8 0.0 copy-start.4
  39.8 14.2 %all_to_all.27 = f32[64,8,128]{2,1,0:T(8,128)S(1)} all-to-all(f32[64,8,128]{2,1,0:T(8,128)S(1)} %bitcast.20), channel_id=1, replica_groups=mesh['half'=2,'pair'=2,'core'=2,'gy'=16] {'gy','pair','core'}, dimensions={0} | all-to-all | bytes 524288 | tf_op jit(solution)/shard_map/all_to_all | solution.py:382
  54.1 1.1 %shard_map.73 = f32[1088,128]{1,0:T(8,128)S(1)} custom-call(f32[512,128]{1,0:T(8,128)S(1)} %bitcast.17, f32[1024,128]{1,0:T(8,128)S(1)} %bitcast.12, f32[512,128]{1,0:T(8,128)S(1)} %get-tuple-element.11.old, f32[2,16,128]{2,1,0:T(8,128)S(1)} %get-tuple-element.10.ends.old_ends, f32[2,16,128]{2,1,0:T(8,128)S(1)} %collective-permute-done.1.sibling, ...), custom_call_target="tpu_custom_call" | custom-call | tf_op jit(solution)/shard_map/pallas_call | solution.py:415
  55.2 13.9 %all_to_all.28 = f32[8,136,128]{2,1,0:T(8,128)S(1)} all-to-all(f32[8,136,128]{2,1,0:T(8,128)S(1)} %bitcast.15), channel_id=1, replica_groups=mesh['half'=2,'pair'=2,'core'=2,'gy'=16] {'half','pair','core'}, dimensions={0} | all-to-all | bytes 1114112 | tf_op jit(solution)/shard_map/all_to_all | solution.py:382
  69.1 10.9 %all_to_all.29 = f32[16,8,128]{2,1,0:T(8,128)S(1)} all-to-all(f32[16,8,128]{2,1,0:T(8,128)S(1)} %bitcast.22), channel_id=1, replica_groups=mesh['half'=2,'pair'=2,'core'=2,'gy'=16] {'gy'}, dimensions={0} | all-to-all | bytes 131072 | tf_op jit(solution)/shard_map/all_to_all | solution.py:382
  79.9 0.0 copy-done.2
  79.9 0.0 copy-done.3
  79.9 0.0 copy-done.4
  79.9 1.2 %shard_map.75 = (f32[2,256,128]{2,1,0:T(8,128)}, f32[2,256,128]{2,1,0:T(8,128)}) custom-call(f32[1088,128]{1,0:T(8,128)S(1)} %bitcast.14, f32[128,128]{1,0:T(8,128)S(1)} %bitcast.21, f32[2,256,128]{2,1,0:T(8,128)S(1)} %copy-done.2, f32[256,128]{1,0:T(8,128)S(1)} %copy-done.3, f32[256,128]{1,0:T(8,128)S(1)} %copy-done.4), custom_call_target="tpu_custom_call" | custom-call | tf_op jit(solution)/shard_map/pallas_call | solution.py:421
  (5 shorter events, 0.1 us)
Async XLA Ops:
  0.6 17.1 %copy-start.1 = (f32[4,16,128]{2,1,0:T(8,128)S(1)}, f32[4,16,128]{2,1,0:T(8,128)}, u32[]{:S(2)}) copy-start(f32[4,16,128]{2,1,0:T(8,128)} %constant.20.clone.waves) | copy-start | bytes 98308
  0.7 17.1 %copy-start = (bf16[16,2,256,256]{3,2,1,0:T(8,128)(2,1)S(1)}, bf16[16,2,256,256]{3,2,1,0:T(8,128)(2,1)}, u32[]{:S(2)}) copy-start(bf16[16,2,256,256]{3,2,1,0:T(8,128)(2,1)} %constant.19.clone.table) | copy-start | bytes 12582916
  18.3 1.3 %collective-permute-start = (f32[2,16,128]{2,1,0:T(8,128)S(1)}, f32[2,16,128]{2,1,0:T(8,128)S(1)}, u32[]{:S(2)}, u32[]{:S(2)}) collective-permute-start(f32[2,16,128]{2,1,0:T(8,128)S(1)} %get-tuple-element.8.ends.old_ends), channel_id=1, source_target_pairs={{0,16},{16,0},{1,17},{17,1},{2,18},{18,2},{3,19},{19,3},{4,20},{20... | collective-permute-start | bytes 49160 | tf_op jit(solution)/shard_map/ppermute | solution.py:396
  38.5 1.3 %collective-permute-start.1 = (f32[2,16,128]{2,1,0:T(8,128)S(1)}, f32[2,16,128]{2,1,0:T(8,128)S(1)}, u32[]{:S(2)}, u32[]{:S(2)}) collective-permute-start(f32[2,16,128]{2,1,0:T(8,128)S(1)} %get-tuple-element.10.ends.old_ends), channel_id=1, source_target_pairs={{0,16},{16,0},{1,17},{17,1},{2,18},{18,2},{3,19},{19,3},{4,20},{20... | collective-permute-start | bytes 49160 | tf_op jit(solution)/shard_map/ppermute | solution.py:396
  39.8 40.1 %copy-start.2 = (f32[2,256,128]{2,1,0:T(8,128)S(1)}, f32[2,256,128]{2,1,0:T(8,128)}, u32[]{:S(2)}) copy-start(f32[2,256,128]{2,1,0:T(8,128)} %sources.3) | copy-start | bytes 786436
  39.8 40.1 %copy-start.3 = (f32[256,128]{1,0:T(8,128)S(1)}, f32[256,128]{1,0:T(8,128)}, u32[]{:S(2)}) copy-start(f32[256,128]{1,0:T(8,128)} %metric.3) | copy-start | bytes 393220
  39.8 40.1 %copy-start.4 = (f32[256,128]{1,0:T(8,128)S(1)}, f32[256,128]{1,0:T(8,128)}, u32[]{:S(2)}) copy-start(f32[256,128]{1,0:T(8,128)} %helm.3) | copy-start | bytes 393220

commit v5 on v4

--- a/solution.py
+++ b/solution.py
@@ -146,21 +146,22 @@
 
 def leave_block(sources, metric, helm, table, waves, here, core, sent, source_here, metric_here, helm_here, arrived):
     moves = [(metric, metric_here)]
-    moves += [(sources.at[f], source_here.at[f]) for f in range(2)] + [(helm, helm_here)]
+    moves += [(sources, source_here), (helm, helm_here)]
     copies = [pltpu.make_async_copy(a, b, arrived.at[n]) for n, (a, b) in enumerate(moves)]
     for copy in copies:
         copy.start()
     copies[0].wait()
     inverse = 1.0 / metric_here[...]
     for f in range(2):
-        copies[1 + f].wait()
+        if f == 0:
+            copies[1].wait()
         field = source_here[f] * inverse
         for h in range(2):
             across = field[LANES * h : LANES * (h + 1), :].T
             for quarter in range(4):
                 rows = pl.ds(LANES * (4 * f + quarter) + h, BLOCK, stride=2)
                 sent[rows, :] = across[BLOCK * quarter : BLOCK * (quarter + 1)]
-    copies[3].wait()
+    copies[2].wait()
     weight = helm_here[...] * (inverse * inverse) - SHIFT
     for h in range(2):
         across = weight[LANES * h : LANES * (h + 1), :].T
@@ -291,22 +292,19 @@
             wz, wh = weight * z1, weight * h
             for q, (one, two) in enumerate(((u1, z1), (u1, h), (g, z1), (g, h), (wz, z1), (wz, h), (wh, h))):
                 sums[q] += one * two
-            place = 136 * (a // 2) + 16 * chunk + a % 2
+            place = 130 * (a // 2) + 16 * chunk + a % 2
             sent[pl.ds(place, 8, stride=2), :] = before
             sent[pl.ds(place + 64, 8, stride=2), :] = new
-    lane = lax.broadcasted_iota(jnp.int32, (8, LANES), 1)
+    lane = lax.broadcasted_iota(jnp.int32, (2, LANES), 1)
     line = jnp.where(lane == 7, n0, jnp.where(lane == 8, n1, jnp.where(lane == 9, step, 0.0)))
     for q in range(7):
         line = jnp.where(lane == q, jnp.sum(sums[q], axis=(0, 1), keepdims=True), line)
     for i in range(8):
-        sent[pl.ds(136 * i + 128, 8), :] = line
+        sent[pl.ds(130 * i + 128, 2), :] = line
 
 
 def gather_sums(received, sent):
-    row = lax.broadcasted_iota(jnp.int32, (8, LANES), 0)
-    rows = received[pl.ds(128, 8), :]
-    for i in range(1, 8):
-        rows = jnp.where(row == i, received[pl.ds(136 * i + 128, 8), :], rows)
+    rows = received[pl.ds(128, 8, stride=130), :]
     for n in range(16):
         sent[pl.ds(8 * n, 8), :] = rows
 
@@ -343,17 +341,16 @@
         for h in range(2):
             pair = []
             for field in range(2):
-                places = [136 * (4 * f + quarter) + 64 * field + h for quarter in range(4)]
+                places = [130 * (4 * f + quarter) + 64 * field + h for quarter in range(4)]
                 columns = [received[pl.ds(place, BLOCK, stride=2), :] for place in places]
                 pair.append(jnp.concatenate(columns, axis=0).T)
             old, new = pair
             rows = slice(LANES * h, LANES * (h + 1))
             near[0, f, rows, :] = (c0 * old + c1 * new) * inverse[rows]
             near[1, f, rows, :] = (1.0 - c0) * sources[f, rows, :] - ((c0 + c1) * old + c1 * new) * weight[rows]
-            for n, out in enumerate((solution, resid)):
-                place = (f, pl.ds(LANES * h, LANES))
-                copies.append(pltpu.make_async_copy(near.at[n, *place], out.at[*place], done.at[4 * n + 2 * f + h]))
-                copies[-1].start()
+        for n, out in enumerate((solution, resid)):
+            copies.append(pltpu.make_async_copy(near.at[n, f], out.at[f], done.at[2 * n + f]))
+            copies[-1].start()
     for copy in copies:
         copy.wait()
 
@@ -412,16 +409,16 @@
     twin = swap(more)
     (sent,) = call(leave_lines, [SENT], [])(more, twin, waves, here, core)
     received = exchange(sent, column, 64, 8)
-    (sent,) = call(pencil_last, [(8 * 136, LANES)], [RS, LINES])(
+    (sent,) = call(pencil_last, [(8 * 130, LANES)], [RS, LINES])(
         received, blocks, second, more, twin, kept, sums, table, waves, here, core
     )
-    received = exchange(sent, line, 8, 136)
+    received = exchange(sent, line, 8, 65, 2)
     (parts,) = call(gather_sums, [(LANES, LANES)], [])(received)
     parts = exchange(parts, "gy", 16, 8)
     outs = call(
         enter_block,
         [sources.shape] * 2,
-        [pltpu.VMEM((2, *sources.shape), jnp.float32), pltpu.SemaphoreType.DMA((8,))],
+        [pltpu.VMEM((2, *sources.shape), jnp.float32), pltpu.SemaphoreType.DMA((4,))],
         in_specs=[vmem] * 5,
         out_specs=[hbm] * 2,
     )(received, parts, sources, metric, helm)

time: 81.4 us -> 81.2 us (level)
  no operation moved by 1% of the time
where the time goes in v5:
time: 81.2 us; the launch traced here: 80.9 us
  blocking collectives  71.9 us (89%)
  Pallas kernels  5.73 us (7%)
  waiting for transfers between devices  2.27 us (3%)
    all_to_all x5, blocking collectives, exchange(): moved = lax.all_to_all(flat.reshape(*shape, LANES), axes, 0, 0, tiled=True)  71.9 us
    ppermute x2, waiting for transfers between devices, swap(): return lax.ppermute(ends, 'core', [(0, 1), (1, 0)])  2.27 us
  transfers between devices with their start and end apart: 2, of which 2 were waited for; matrix products, arithmetic and copies ran while one was open for 0% of the time, Pallas kernels for 0%

profile of v5, /device:TPU:0, one launch (start us, length us, event | category | flops | bytes accessed | tf_op | source)
XLA Modules:
  0.0 80.9 jit_solution(13915857546877973178)
XLA Ops:
  0.6 0.0 copy-start.1
  0.7 0.0 copy-start
  0.7 1.4 %shard_map.68 = f32[1024,128]{1,0:T(8,128)S(1)} custom-call(f32[2,256,128]{2,1,0:T(8,128)} %sources.3, f32[256,128]{1,0:T(8,128)} %metric.3, f32[256,128]{1,0:T(8,128)} %helm.3, bf16[16,2,256,256]{3,2,1,0:T(8,128)(2,1)} %constant.19.clone.table, f32[4,16,128]{2,1,0:T(8,128)} %constant.20.clone.waves, f32[1,128]{1,0:T(1,128)S(1)} %broadcast_in_dim.6.here, ...), custom_call_target="tpu_custom_call" | custom-call | tf_op jit(solution)/shard_map/pallas_call | solution.py:395
  2.1 15.6 %all_to_all.25 = f32[8,128,128]{2,1,0:T(8,128)S(1)} all-to-all(f32[8,128,128]{2,1,0:T(8,128)S(1)} %bitcast.16), channel_id=1, replica_groups=mesh['half'=2,'pair'=2,'core'=2,'gy'=16] {'half','pair','core'}, dimensions={0} | all-to-all | bytes 1048576 | tf_op jit(solution)/shard_map/all_to_all | solution.py:379
  17.7 0.0 copy-done.1
  17.7 0.0 copy-done
  17.7 0.6 shard_map.69
  18.3 0.1 collective-permute-start
  18.4 1.2 %collective-permute-done.sibling = f32[2,16,128]{2,1,0:T(8,128)S(1)} collective-permute-done((f32[2,16,128]{2,1,0:T(8,128)S(1)}, f32[2,16,128]{2,1,0:T(8,128)S(1)}, u32[]{:S(2)}, u32[]{:S(2)}) %collective-permute-start) | collective-permute-done | bytes 16416 | tf_op jit(solution)/shard_map/ppermute | solution.py:393
  19.6 17.5 %all_to_all.26 = f32[64,8,128]{2,1,0:T(8,128)S(1)} all-to-all(f32[64,8,128]{2,1,0:T(8,128)S(1)} %bitcast.19), channel_id=1, replica_groups=mesh['half'=2,'pair'=2,'core'=2,'gy'=16] {'gy','pair','core'}, dimensions={0} | all-to-all | bytes 524288 | tf_op jit(solution)/shard_map/all_to_all | solution.py:379
  37.2 1.4 %shard_map.71 = (f32[512,128]{1,0:T(8,128)S(1)}, f32[2,16,128]{2,1,0:T(8,128)S(1)}, f32[16,32,128]{2,1,0:T(8,128)S(1)}, f32[2,8,128]{2,1,0:T(8,128)S(1)}) custom-call(f32[512,128]{1,0:T(8,128)S(1)} %bitcast.18, f32[1024,128]{1,0:T(8,128)S(1)} %bitcast.11, f32[512,128]{1,0:T(8,128)S(1)} %get-tuple-element.9.old, ...), custom_call_target="tpu_custom_call" | custom-call | tf_op jit(solution)/shard_map/pallas_call | solution.py:406
  38.5 0.2 collective-permute-start.1
  38.7 1.1 %collective-permute-done.1.sibling = f32[2,16,128]{2,1,0:T(8,128)S(1)} collective-permute-done((f32[2,16,128]{2,1,0:T(8,128)S(1)}, f32[2,16,128]{2,1,0:T(8,128)S(1)}, u32[]{:S(2)}, u32[]{:S(2)}) %collective-permute-start.1) | collective-permute-done | bytes 16416 | tf_op jit(solution)/shard_map/ppermute | solution.py:393
  39.8 0.0 copy-start.2
  39.8 0.0 copy-start.3
  39.9 0.0 copy-start.4
  39.9 14.2 %all_to_all.27 = f32[64,8,128]{2,1,0:T(8,128)S(1)} all-to-all(f32[64,8,128]{2,1,0:T(8,128)S(1)} %bitcast.20), channel_id=1, replica_groups=mesh['half'=2,'pair'=2,'core'=2,'gy'=16] {'gy','pair','core'}, dimensions={0} | all-to-all | bytes 524288 | tf_op jit(solution)/shard_map/all_to_all | solution.py:379
  54.1 1.1 %shard_map.73 = f32[1040,128]{1,0:T(8,128)S(1)} custom-call(f32[512,128]{1,0:T(8,128)S(1)} %bitcast.17, f32[1024,128]{1,0:T(8,128)S(1)} %bitcast.12, f32[512,128]{1,0:T(8,128)S(1)} %get-tuple-element.11.old, f32[2,16,128]{2,1,0:T(8,128)S(1)} %get-tuple-element.10.ends.old_ends, f32[2,16,128]{2,1,0:T(8,128)S(1)} %collective-permute-done.1.sibling, ...), custom_call_target="tpu_custom_call" | custom-call | tf_op jit(solution)/shard_map/pallas_call | solution.py:412
  55.2 13.7 %all_to_all.28 = f32[8,65,2,128]{3,2,1,0:T(2,128)S(1)} all-to-all(f32[8,65,2,128]{3,2,1,0:T(2,128)S(1)} %bitcast.15), channel_id=1, replica_groups=mesh['half'=2,'pair'=2,'core'=2,'gy'=16] {'half','pair','core'}, dimensions={0} | all-to-all | bytes 1064960 | tf_op jit(solution)/shard_map/all_to_all | solution.py:379
  68.8 10.8 %all_to_all.29 = f32[16,8,128]{2,1,0:T(8,128)S(1)} all-to-all(f32[16,8,128]{2,1,0:T(8,128)S(1)} %bitcast.22), channel_id=1, replica_groups=mesh['half'=2,'pair'=2,'core'=2,'gy'=16] {'gy'}, dimensions={0} | all-to-all | bytes 131072 | tf_op jit(solution)/shard_map/all_to_all | solution.py:379
  79.7 0.0 copy-done.2
  79.7 0.0 copy-done.3
  79.7 0.0 copy-done.4
  79.7 1.2 %shard_map.75 = (f32[2,256,128]{2,1,0:T(8,128)}, f32[2,256,128]{2,1,0:T(8,128)}) custom-call(f32[1040,128]{1,0:T(8,128)S(1)} %bitcast.14, f32[128,128]{1,0:T(8,128)S(1)} %bitcast.21, f32[2,256,128]{2,1,0:T(8,128)S(1)} %copy-done.2, f32[256,128]{1,0:T(8,128)S(1)} %copy-done.3, f32[256,128]{1,0:T(8,128)S(1)} %copy-done.4), custom_call_target="tpu_custom_call" | custom-call | tf_op jit(solution)/shard_map/pallas_call | solution.py:418
  (5 shorter events, 0.1 us)
Async XLA Ops:
  0.6 17.1 %copy-start.1 = (f32[4,16,128]{2,1,0:T(8,128)S(1)}, f32[4,16,128]{2,1,0:T(8,128)}, u32[]{:S(2)}) copy-start(f32[4,16,128]{2,1,0:T(8,128)} %constant.20.clone.waves) | copy-start | bytes 98308
  0.7 17.1 %copy-start = (bf16[16,2,256,256]{3,2,1,0:T(8,128)(2,1)S(1)}, bf16[16,2,256,256]{3,2,1,0:T(8,128)(2,1)}, u32[]{:S(2)}) copy-start(bf16[16,2,256,256]{3,2,1,0:T(8,128)(2,1)} %constant.19.clone.table) | copy-start | bytes 12582916
  18.3 1.3 %collective-permute-start = (f32[2,16,128]{2,1,0:T(8,128)S(1)}, f32[2,16,128]{2,1,0:T(8,128)S(1)}, u32[]{:S(2)}, u32[]{:S(2)}) collective-permute-start(f32[2,16,128]{2,1,0:T(8,128)S(1)} %get-tuple-element.8.ends.old_ends), channel_id=1, source_target_pairs={{0,16},{16,0},{1,17},{17,1},{2,18},{18,2},{3,19},{19,3},{4,20},{20... | collective-permute-start | bytes 49160 | tf_op jit(solution)/shard_map/ppermute | solution.py:393
  38.5 1.3 %collective-permute-start.1 = (f32[2,16,128]{2,1,0:T(8,128)S(1)}, f32[2,16,128]{2,1,0:T(8,128)S(1)}, u32[]{:S(2)}, u32[]{:S(2)}) collective-permute-start(f32[2,16,128]{2,1,0:T(8,128)S(1)} %get-tuple-element.10.ends.old_ends), channel_id=1, source_target_pairs={{0,16},{16,0},{1,17},{17,1},{2,18},{18,2},{3,19},{19,3},{4,20},{20... | collective-permute-start | bytes 49160 | tf_op jit(solution)/shard_map/ppermute | solution.py:393
  39.8 39.9 %copy-start.2 = (f32[2,256,128]{2,1,0:T(8,128)S(1)}, f32[2,256,128]{2,1,0:T(8,128)}, u32[]{:S(2)}) copy-start(f32[2,256,128]{2,1,0:T(8,128)} %sources.3) | copy-start | bytes 786436
  39.8 39.9 %copy-start.3 = (f32[256,128]{1,0:T(8,128)S(1)}, f32[256,128]{1,0:T(8,128)}, u32[]{:S(2)}) copy-start(f32[256,128]{1,0:T(8,128)} %metric.3) | copy-start | bytes 393220
  39.9 39.8 %copy-start.4 = (f32[256,128]{1,0:T(8,128)S(1)}, f32[256,128]{1,0:T(8,128)}, u32[]{:S(2)}) copy-start(f32[256,128]{1,0:T(8,128)} %helm.3) | copy-start | bytes 393220

commit v6 on v5

--- a/solution.py
+++ b/solution.py
@@ -144,35 +144,37 @@
     return R, S
 
 
+def place_of(half, quarter):
+    return 2 * quarter + half
+
+
 def leave_block(sources, metric, helm, table, waves, here, core, sent, source_here, metric_here, helm_here, arrived):
-    moves = [(metric, metric_here)]
-    moves += [(sources, source_here), (helm, helm_here)]
+    moves = [(metric, metric_here), (helm, helm_here), (sources, source_here)]
     copies = [pltpu.make_async_copy(a, b, arrived.at[n]) for n, (a, b) in enumerate(moves)]
     for copy in copies:
         copy.start()
     copies[0].wait()
     inverse = 1.0 / metric_here[...]
-    for f in range(2):
-        if f == 0:
-            copies[1].wait()
-        field = source_here[f] * inverse
-        for h in range(2):
-            across = field[LANES * h : LANES * (h + 1), :].T
-            for quarter in range(4):
-                rows = pl.ds(LANES * (4 * f + quarter) + h, BLOCK, stride=2)
-                sent[rows, :] = across[BLOCK * quarter : BLOCK * (quarter + 1)]
-    copies[2].wait()
+    copies[1].wait()
     weight = helm_here[...] * (inverse * inverse) - SHIFT
     for h in range(2):
         across = weight[LANES * h : LANES * (h + 1), :].T
         for quarter in range(4):
             for f in range(2):
-                rows = pl.ds(LANES * (4 * f + quarter) + 64 + h, BLOCK, stride=2)
+                rows = pl.ds(LANES * place_of(f, quarter) + 64 + h, BLOCK, stride=2)
                 sent[rows, :] = across[BLOCK * quarter : BLOCK * (quarter + 1)]
+    copies[2].wait()
+    for f in range(2):
+        field = source_here[f] * inverse
+        for h in range(2):
+            across = field[LANES * h : LANES * (h + 1), :].T
+            for quarter in range(4):
+                rows = pl.ds(LANES * place_of(f, quarter) + h, BLOCK, stride=2)
+                sent[rows, :] = across[BLOCK * quarter : BLOCK * (quarter + 1)]
 
 
 def from_block(blocks, a, chunk, field):
-    return blocks[pl.ds(LANES * (a // 2) + 64 * field + 16 * chunk + a % 2, 8, stride=2), :]
+    return blocks[pl.ds(LANES * place_of(a // 8, a // 2 % 4) + 64 * field + 16 * chunk + a % 2, 8, stride=2), :]
 
 
 def lines(spectrum, y):
@@ -224,12 +226,16 @@
     rho, decay, scale, rounds = waves[0], waves[1], waves[2], waves[3]
     whole, double = jnp.exp(-decay), jnp.exp(-2.0 * decay)
     b = here[...]
-    low = jnp.zeros((16, LANES), jnp.float32)
-    high = jnp.zeros((16, LANES), jnp.float32)
-    for n in range(BLOCKS):
-        low = jnp.where(b > n, received[pl.ds(16 * n, 16), :] + double * low, low)
-        m = BLOCKS - 1 - n
-        high = jnp.where(b < m, received[pl.ds(16 * m, 16), :] + double * high, high)
+    middle = BLOCKS // 2
+    low, high = [[jnp.zeros((16, LANES), jnp.float32)] * 2 for _ in range(2)]
+    for n in range(middle):
+        for part in range(2):
+            k = n + middle * part
+            low[part] = jnp.where(b > k, received[pl.ds(16 * k, 16), :] + double * low[part], low[part])
+            m = BLOCKS - 1 - k
+            high[part] = jnp.where(b < m, received[pl.ds(16 * m, 16), :] + double * high[part], high[part])
+    low = low[1] + jnp.exp(-2.0 * decay * jnp.maximum(b - middle, 0.0)) * low[0]
+    high = high[1] + jnp.exp(-2.0 * decay * jnp.maximum(middle - 1.0 - b, 0.0)) * high[0]
     upper = core[...] > 0
     p, q = both_cores(ends, sibling, whole, upper)
     left = jnp.exp(-decay * (4.0 * b))
@@ -292,11 +298,11 @@
             wz, wh = weight * z1, weight * h
             for q, (one, two) in enumerate(((u1, z1), (u1, h), (g, z1), (g, h), (wz, z1), (wz, h), (wh, h))):
                 sums[q] += one * two
-            place = 130 * (a // 2) + 16 * chunk + a % 2
+            place = 130 * place_of(a // 8, a // 2 % 4) + 16 * chunk + a % 2
             sent[pl.ds(place, 8, stride=2), :] = before
             sent[pl.ds(place + 64, 8, stride=2), :] = new
     lane = lax.broadcasted_iota(jnp.int32, (2, LANES), 1)
-    line = jnp.where(lane == 7, n0, jnp.where(lane == 8, n1, jnp.where(lane == 9, step, 0.0)))
+    line = jnp.where(lane == 7, n0, jnp.where(lane == 8, n1, jnp.where(lane >= 64, step, 0.0)))
     for q in range(7):
         line = jnp.where(lane == q, jnp.sum(sums[q], axis=(0, 1), keepdims=True), line)
     for i in range(8):
@@ -314,7 +320,7 @@
     lane = lax.broadcasted_iota(jnp.int32, (1, LANES), 1)
     row = lax.broadcasted_iota(jnp.int32, (LANES, LANES), 0)
     every = parts[...]
-    steps = jnp.sum(jnp.where(lane == 9, every, 0.0), axis=1, keepdims=True)
+    steps = pltpu.roll(every, 64, 1)
 
     def pick(line, q):
         return jnp.sum(jnp.where(lane == q, line, 0.0), axis=1, keepdims=True)
@@ -323,7 +329,7 @@
     inverse = 1.0 / m
     weight = helm[...] * inverse - SHIFT * m
     for f in range(2):
-        mine = jnp.where(row % 8 // 4 == f, every, 0.0)
+        mine = jnp.where(row % 2 == f, every, 0.0)
         zeroth = jnp.sum(mine, axis=0, keepdims=True)
         n0, n1 = pick(zeroth, 7), pick(zeroth, 8)
         delta = n0 + n1
@@ -341,7 +347,7 @@
         for h in range(2):
             pair = []
             for field in range(2):
-                places = [130 * (4 * f + quarter) + 64 * field + h for quarter in range(4)]
+                places = [130 * place_of(f, quarter) + 64 * field + h for quarter in range(4)]
                 columns = [received[pl.ds(place, BLOCK, stride=2), :] for place in places]
                 pair.append(jnp.concatenate(columns, axis=0).T)
             old, new = pair
@@ -382,7 +388,7 @@
 
 def per_device(sources, metric, helm):
     table, waves = (jnp.asarray(a) for a in tables())
-    line, column = ("half", "pair", "core"), ("gy", "pair", "core")
+    line, column = ("pair", "core", "half"), ("gy", "pair", "core")
     here = lax.axis_index("gy") * lax.axis_size("pair") + lax.axis_index("pair")
     here = jnp.full((1, LANES), here, jnp.float32)
     core = jnp.full((1, LANES), lax.axis_index("core"), jnp.float32)

time: 81.2 us -> 80.7 us (level)
  no operation moved by 1% of the time
where the time goes in v6:
time: 80.7 us; the launch traced here: 80.5 us
  blocking collectives  71.3 us (88%)
  Pallas kernels  5.69 us (7%)
  waiting for transfers between devices  1.93 us (2%)
    all_to_all x5, blocking collectives, exchange(): moved = lax.all_to_all(flat.reshape(*shape, LANES), axes, 0, 0, tiled=True)  71.3 us
    ppermute x2, waiting for transfers between devices, swap(): return lax.ppermute(ends, 'core', [(0, 1), (1, 0)])  1.93 us
  transfers between devices with their start and end apart: 2, of which 2 were waited for; matrix products, arithmetic and copies ran while one was open for 0% of the time, Pallas kernels for 0%

profile of v6, /device:TPU:0, one launch (start us, length us, event | category | flops | bytes accessed | tf_op | source)
XLA Modules:
  0.0 80.5 jit_solution(13265643848695208244)
XLA Ops:
  0.6 0.0 copy-start.1
  0.7 0.0 copy-start
  0.7 1.4 %shard_map.68 = f32[1024,128]{1,0:T(8,128)S(1)} custom-call(f32[2,256,128]{2,1,0:T(8,128)} %sources.3, f32[256,128]{1,0:T(8,128)} %metric.3, f32[256,128]{1,0:T(8,128)} %helm.3, bf16[16,2,256,256]{3,2,1,0:T(8,128)(2,1)} %constant.19.clone.table, f32[4,16,128]{2,1,0:T(8,128)} %constant.20.clone.waves, f32[1,128]{1,0:T(1,128)S(1)} %broadcast_in_dim.6.here, ...), custom_call_target="tpu_custom_call" | custom-call | tf_op jit(solution)/shard_map/pallas_call | solution.py:401
  2.1 14.7 %all_to_all.25 = f32[8,128,128]{2,1,0:T(8,128)S(1)} all-to-all(f32[8,128,128]{2,1,0:T(8,128)S(1)} %bitcast.16), channel_id=1, replica_groups=mesh['half'=2,'pair'=2,'core'=2,'gy'=16] {'pair','core','half'}, dimensions={0} | all-to-all | bytes 1048576 | tf_op jit(solution)/shard_map/all_to_all | solution.py:385
  16.8 0.0 copy-done.1
  16.8 0.0 copy-done
  16.8 0.6 shard_map.69
  17.4 0.6 collective-permute-start
  18.0 0.8 %collective-permute-done.sibling = f32[2,16,128]{2,1,0:T(8,128)S(1)} collective-permute-done((f32[2,16,128]{2,1,0:T(8,128)S(1)}, f32[2,16,128]{2,1,0:T(8,128)S(1)}, u32[]{:S(2)}, u32[]{:S(2)}) %collective-permute-start) | collective-permute-done | bytes 16416 | tf_op jit(solution)/shard_map/ppermute | solution.py:399
  18.9 17.5 %all_to_all.26 = f32[64,8,128]{2,1,0:T(8,128)S(1)} all-to-all(f32[64,8,128]{2,1,0:T(8,128)S(1)} %bitcast.19), channel_id=1, replica_groups=mesh['half'=2,'pair'=2,'core'=2,'gy'=16] {'gy','pair','core'}, dimensions={0} | all-to-all | bytes 524288 | tf_op jit(solution)/shard_map/all_to_all | solution.py:385
  36.4 1.3 %shard_map.71 = (f32[512,128]{1,0:T(8,128)S(1)}, f32[2,16,128]{2,1,0:T(8,128)S(1)}, f32[16,32,128]{2,1,0:T(8,128)S(1)}, f32[2,8,128]{2,1,0:T(8,128)S(1)}) custom-call(f32[512,128]{1,0:T(8,128)S(1)} %bitcast.18, f32[1024,128]{1,0:T(8,128)S(1)} %bitcast.11, f32[512,128]{1,0:T(8,128)S(1)} %get-tuple-element.9.old, ...), custom_call_target="tpu_custom_call" | custom-call | tf_op jit(solution)/shard_map/pallas_call | solution.py:412
  37.7 0.2 collective-permute-start.1
  37.9 1.1 %collective-permute-done.1.sibling = f32[2,16,128]{2,1,0:T(8,128)S(1)} collective-permute-done((f32[2,16,128]{2,1,0:T(8,128)S(1)}, f32[2,16,128]{2,1,0:T(8,128)S(1)}, u32[]{:S(2)}, u32[]{:S(2)}) %collective-permute-start.1) | collective-permute-done | bytes 16416 | tf_op jit(solution)/shard_map/ppermute | solution.py:399
  39.0 0.0 copy-start.2
  39.1 0.0 copy-start.3
  39.1 0.0 copy-start.4
  39.1 14.2 %all_to_all.27 = f32[64,8,128]{2,1,0:T(8,128)S(1)} all-to-all(f32[64,8,128]{2,1,0:T(8,128)S(1)} %bitcast.20), channel_id=1, replica_groups=mesh['half'=2,'pair'=2,'core'=2,'gy'=16] {'gy','pair','core'}, dimensions={0} | all-to-all | bytes 524288 | tf_op jit(solution)/shard_map/all_to_all | solution.py:385
  53.3 1.1 %shard_map.73 = f32[1040,128]{1,0:T(8,128)S(1)} custom-call(f32[512,128]{1,0:T(8,128)S(1)} %bitcast.17, f32[1024,128]{1,0:T(8,128)S(1)} %bitcast.12, f32[512,128]{1,0:T(8,128)S(1)} %get-tuple-element.11.old, f32[2,16,128]{2,1,0:T(8,128)S(1)} %get-tuple-element.10.ends.old_ends, f32[2,16,128]{2,1,0:T(8,128)S(1)} %collective-permute-done.1.sibling, ...), custom_call_target="tpu_custom_call" | custom-call | tf_op jit(solution)/shard_map/pallas_call | solution.py:418
  54.4 14.0 %all_to_all.28 = f32[8,65,2,128]{3,2,1,0:T(2,128)S(1)} all-to-all(f32[8,65,2,128]{3,2,1,0:T(2,128)S(1)} %bitcast.15), channel_id=1, replica_groups=mesh['half'=2,'pair'=2,'core'=2,'gy'=16] {'pair','core','half'}, dimensions={0} | all-to-all | bytes 1064960 | tf_op jit(solution)/shard_map/all_to_all | solution.py:385
  68.4 10.8 %all_to_all.29 = f32[16,8,128]{2,1,0:T(8,128)S(1)} all-to-all(f32[16,8,128]{2,1,0:T(8,128)S(1)} %bitcast.22), channel_id=1, replica_groups=mesh['half'=2,'pair'=2,'core'=2,'gy'=16] {'gy'}, dimensions={0} | all-to-all | bytes 131072 | tf_op jit(solution)/shard_map/all_to_all | solution.py:385
  79.2 0.0 copy-done.2
  79.2 0.0 copy-done.3
  79.2 0.0 copy-done.4
  79.3 1.2 %shard_map.75 = (f32[2,256,128]{2,1,0:T(8,128)}, f32[2,256,128]{2,1,0:T(8,128)}) custom-call(f32[1040,128]{1,0:T(8,128)S(1)} %bitcast.14, f32[128,128]{1,0:T(8,128)S(1)} %bitcast.21, f32[2,256,128]{2,1,0:T(8,128)S(1)} %copy-done.2, f32[256,128]{1,0:T(8,128)S(1)} %copy-done.3, f32[256,128]{1,0:T(8,128)S(1)} %copy-done.4), custom_call_target="tpu_custom_call" | custom-call | tf_op jit(solution)/shard_map/pallas_call | solution.py:424
  (5 shorter events, 0.1 us)
Async XLA Ops:
  0.6 16.2 %copy-start.1 = (f32[4,16,128]{2,1,0:T(8,128)S(1)}, f32[4,16,128]{2,1,0:T(8,128)}, u32[]{:S(2)}) copy-start(f32[4,16,128]{2,1,0:T(8,128)} %constant.20.clone.waves) | copy-start | bytes 98308
  0.7 16.1 %copy-start = (bf16[16,2,256,256]{3,2,1,0:T(8,128)(2,1)S(1)}, bf16[16,2,256,256]{3,2,1,0:T(8,128)(2,1)}, u32[]{:S(2)}) copy-start(bf16[16,2,256,256]{3,2,1,0:T(8,128)(2,1)} %constant.19.clone.table) | copy-start | bytes 12582916
  17.4 1.4 %collective-permute-start = (f32[2,16,128]{2,1,0:T(8,128)S(1)}, f32[2,16,128]{2,1,0:T(8,128)S(1)}, u32[]{:S(2)}, u32[]{:S(2)}) collective-permute-start(f32[2,16,128]{2,1,0:T(8,128)S(1)} %get-tuple-element.8.ends.old_ends), channel_id=1, source_target_pairs={{0,16},{16,0},{1,17},{17,1},{2,18},{18,2},{3,19},{19,3},{4,20},{20... | collective-permute-start | bytes 49160 | tf_op jit(solution)/shard_map/ppermute | solution.py:399
  37.7 1.3 %collective-permute-start.1 = (f32[2,16,128]{2,1,0:T(8,128)S(1)}, f32[2,16,128]{2,1,0:T(8,128)S(1)}, u32[]{:S(2)}, u32[]{:S(2)}) collective-permute-start(f32[2,16,128]{2,1,0:T(8,128)S(1)} %get-tuple-element.10.ends.old_ends), channel_id=1, source_target_pairs={{0,16},{16,0},{1,17},{17,1},{2,18},{18,2},{3,19},{19,3},{4,20},{20... | collective-permute-start | bytes 49160 | tf_op jit(solution)/shard_map/ppermute | solution.py:399
  39.0 40.2 %copy-start.2 = (f32[2,256,128]{2,1,0:T(8,128)S(1)}, f32[2,256,128]{2,1,0:T(8,128)}, u32[]{:S(2)}) copy-start(f32[2,256,128]{2,1,0:T(8,128)} %sources.3) | copy-start | bytes 786436
  39.1 40.2 %copy-start.3 = (f32[256,128]{1,0:T(8,128)S(1)}, f32[256,128]{1,0:T(8,128)}, u32[]{:S(2)}) copy-start(f32[256,128]{1,0:T(8,128)} %metric.3) | copy-start | bytes 393220
  39.1 40.2 %copy-start.4 = (f32[256,128]{1,0:T(8,128)S(1)}, f32[256,128]{1,0:T(8,128)}, u32[]{:S(2)}) copy-start(f32[256,128]{1,0:T(8,128)} %helm.3) | copy-start | bytes 393220

commit v7 on v6

--- a/solution.py
+++ b/solution.py
@@ -322,8 +322,11 @@
     every = parts[...]
     steps = pltpu.roll(every, 64, 1)
 
+    def total(line):
+        return jnp.sum(line, axis=1, keepdims=True)
+
     def pick(line, q):
-        return jnp.sum(jnp.where(lane == q, line, 0.0), axis=1, keepdims=True)
+        return total(jnp.where(lane == q, line, 0.0))
 
     m = metric[...]
     inverse = 1.0 / m
@@ -338,9 +341,10 @@
         moved = away * mine
         first = jnp.sum(moved, axis=0, keepdims=True)
         second = jnp.sum(away * moved, axis=0, keepdims=True)
-        gamma = pick(zeroth, 0) - (pick(first, 1) + pick(first, 2)) + pick(second, 3)
-        inner = pick(zeroth, 4) - 2.0 * pick(first, 5) + pick(second, 6)
-        cross = pick(zeroth, 2) - pick(first, 3)
+        once = (lane == 1) | (lane == 2)
+        gamma = total(jnp.where(lane == 0, zeroth, jnp.where(once, -first, jnp.where(lane == 3, second, 0.0))))
+        inner = total(jnp.where(lane == 4, zeroth, jnp.where(lane == 5, -2.0 * first, jnp.where(lane == 6, second, 0.0))))
+        cross = total(jnp.where(lane == 2, zeroth, jnp.where(lane == 3, -first, 0.0)))
         beta = gamma / n0
         size = gamma / (gamma + inner + 2.0 * beta * cross + beta * beta * delta)
         c0, c1 = alpha + size * (rest + beta), -size * alpha

time: 80.7 us -> 80.7 us (level)
  no operation moved by 1% of the time
where the time goes in v7:
time: 80.7 us; the launch traced here: 80.4 us
  blocking collectives  71.3 us (88%)
  Pallas kernels  5.68 us (7%)
  waiting for transfers between devices  1.93 us (2%)
    all_to_all x5, blocking collectives, exchange(): moved = lax.all_to_all(flat.reshape(*shape, LANES), axes, 0, 0, tiled=True)  71.3 us
    ppermute x2, waiting for transfers between devices, swap(): return lax.ppermute(ends, 'core', [(0, 1), (1, 0)])  1.93 us
  transfers between devices with their start and end apart: 2, of which 2 were waited for; matrix products, arithmetic and copies ran while one was open for 0% of the time, Pallas kernels for 0%

profile of v7, /device:TPU:0, one launch (start us, length us, event | category | flops | bytes accessed | tf_op | source)
XLA Modules:
  0.0 80.4 jit_solution(13458405235018048874)
XLA Ops:
  0.6 0.0 copy-start.1
  0.7 0.0 copy-start
  0.7 1.4 %shard_map.68 = f32[1024,128]{1,0:T(8,128)S(1)} custom-call(f32[2,256,128]{2,1,0:T(8,128)} %sources.3, f32[256,128]{1,0:T(8,128)} %metric.3, f32[256,128]{1,0:T(8,128)} %helm.3, bf16[16,2,256,256]{3,2,1,0:T(8,128)(2,1)} %constant.19.clone.table, f32[4,16,128]{2,1,0:T(8,128)} %constant.20.clone.waves, f32[1,128]{1,0:T(1,128)S(1)} %broadcast_in_dim.6.here, ...), custom_call_target="tpu_custom_call" | custom-call | tf_op jit(solution)/shard_map/pallas_call | solution.py:405
  2.1 14.7 %all_to_all.25 = f32[8,128,128]{2,1,0:T(8,128)S(1)} all-to-all(f32[8,128,128]{2,1,0:T(8,128)S(1)} %bitcast.16), channel_id=1, replica_groups=mesh['half'=2,'pair'=2,'core'=2,'gy'=16] {'pair','core','half'}, dimensions={0} | all-to-all | bytes 1048576 | tf_op jit(solution)/shard_map/all_to_all | solution.py:389
  16.8 0.0 copy-done.1
  16.8 0.0 copy-done
  16.8 0.6 shard_map.69
  17.4 0.6 collective-permute-start
  18.0 0.8 %collective-permute-done.sibling = f32[2,16,128]{2,1,0:T(8,128)S(1)} collective-permute-done((f32[2,16,128]{2,1,0:T(8,128)S(1)}, f32[2,16,128]{2,1,0:T(8,128)S(1)}, u32[]{:S(2)}, u32[]{:S(2)}) %collective-permute-start) | collective-permute-done | bytes 16416 | tf_op jit(solution)/shard_map/ppermute | solution.py:403
  18.9 17.5 %all_to_all.26 = f32[64,8,128]{2,1,0:T(8,128)S(1)} all-to-all(f32[64,8,128]{2,1,0:T(8,128)S(1)} %bitcast.19), channel_id=1, replica_groups=mesh['half'=2,'pair'=2,'core'=2,'gy'=16] {'gy','pair','core'}, dimensions={0} | all-to-all | bytes 524288 | tf_op jit(solution)/shard_map/all_to_all | solution.py:389
  36.4 1.3 %shard_map.71 = (f32[512,128]{1,0:T(8,128)S(1)}, f32[2,16,128]{2,1,0:T(8,128)S(1)}, f32[16,32,128]{2,1,0:T(8,128)S(1)}, f32[2,8,128]{2,1,0:T(8,128)S(1)}) custom-call(f32[512,128]{1,0:T(8,128)S(1)} %bitcast.18, f32[1024,128]{1,0:T(8,128)S(1)} %bitcast.11, f32[512,128]{1,0:T(8,128)S(1)} %get-tuple-element.9.old, ...), custom_call_target="tpu_custom_call" | custom-call | tf_op jit(solution)/shard_map/pallas_call | solution.py:416
  37.7 0.2 collective-permute-start.1
  37.9 1.1 %collective-permute-done.1.sibling = f32[2,16,128]{2,1,0:T(8,128)S(1)} collective-permute-done((f32[2,16,128]{2,1,0:T(8,128)S(1)}, f32[2,16,128]{2,1,0:T(8,128)S(1)}, u32[]{:S(2)}, u32[]{:S(2)}) %collective-permute-start.1) | collective-permute-done | bytes 16416 | tf_op jit(solution)/shard_map/ppermute | solution.py:403
  39.0 0.0 copy-start.2
  39.1 0.0 copy-start.3
  39.1 0.0 copy-start.4
  39.1 14.2 %all_to_all.27 = f32[64,8,128]{2,1,0:T(8,128)S(1)} all-to-all(f32[64,8,128]{2,1,0:T(8,128)S(1)} %bitcast.20), channel_id=1, replica_groups=mesh['half'=2,'pair'=2,'core'=2,'gy'=16] {'gy','pair','core'}, dimensions={0} | all-to-all | bytes 524288 | tf_op jit(solution)/shard_map/all_to_all | solution.py:389
  53.3 1.1 %shard_map.73 = f32[1040,128]{1,0:T(8,128)S(1)} custom-call(f32[512,128]{1,0:T(8,128)S(1)} %bitcast.17, f32[1024,128]{1,0:T(8,128)S(1)} %bitcast.12, f32[512,128]{1,0:T(8,128)S(1)} %get-tuple-element.11.old, f32[2,16,128]{2,1,0:T(8,128)S(1)} %get-tuple-element.10.ends.old_ends, f32[2,16,128]{2,1,0:T(8,128)S(1)} %collective-permute-done.1.sibling, ...), custom_call_target="tpu_custom_call" | custom-call | tf_op jit(solution)/shard_map/pallas_call | solution.py:422
  54.4 14.0 %all_to_all.28 = f32[8,65,2,128]{3,2,1,0:T(2,128)S(1)} all-to-all(f32[8,65,2,128]{3,2,1,0:T(2,128)S(1)} %bitcast.15), channel_id=1, replica_groups=mesh['half'=2,'pair'=2,'core'=2,'gy'=16] {'pair','core','half'}, dimensions={0} | all-to-all | bytes 1064960 | tf_op jit(solution)/shard_map/all_to_all | solution.py:389
  68.4 10.8 %all_to_all.29 = f32[16,8,128]{2,1,0:T(8,128)S(1)} all-to-all(f32[16,8,128]{2,1,0:T(8,128)S(1)} %bitcast.22), channel_id=1, replica_groups=mesh['half'=2,'pair'=2,'core'=2,'gy'=16] {'gy'}, dimensions={0} | all-to-all | bytes 131072 | tf_op jit(solution)/shard_map/all_to_all | solution.py:389
  79.2 0.0 copy-done.2
  79.2 0.0 copy-done.3
  79.2 0.0 copy-done.4
  79.3 1.2 %shard_map.75 = (f32[2,256,128]{2,1,0:T(8,128)}, f32[2,256,128]{2,1,0:T(8,128)}) custom-call(f32[1040,128]{1,0:T(8,128)S(1)} %bitcast.14, f32[128,128]{1,0:T(8,128)S(1)} %bitcast.21, f32[2,256,128]{2,1,0:T(8,128)S(1)} %copy-done.2, f32[256,128]{1,0:T(8,128)S(1)} %copy-done.3, f32[256,128]{1,0:T(8,128)S(1)} %copy-done.4), custom_call_target="tpu_custom_call" | custom-call | tf_op jit(solution)/shard_map/pallas_call | solution.py:428
  (5 shorter events, 0.1 us)
Async XLA Ops:
  0.6 16.2 %copy-start.1 = (f32[4,16,128]{2,1,0:T(8,128)S(1)}, f32[4,16,128]{2,1,0:T(8,128)}, u32[]{:S(2)}) copy-start(f32[4,16,128]{2,1,0:T(8,128)} %constant.20.clone.waves) | copy-start | bytes 98308
  0.7 16.1 %copy-start = (bf16[16,2,256,256]{3,2,1,0:T(8,128)(2,1)S(1)}, bf16[16,2,256,256]{3,2,1,0:T(8,128)(2,1)}, u32[]{:S(2)}) copy-start(bf16[16,2,256,256]{3,2,1,0:T(8,128)(2,1)} %constant.19.clone.table) | copy-start | bytes 12582916
  17.4 1.4 %collective-permute-start = (f32[2,16,128]{2,1,0:T(8,128)S(1)}, f32[2,16,128]{2,1,0:T(8,128)S(1)}, u32[]{:S(2)}, u32[]{:S(2)}) collective-permute-start(f32[2,16,128]{2,1,0:T(8,128)S(1)} %get-tuple-element.8.ends.old_ends), channel_id=1, source_target_pairs={{0,16},{16,0},{1,17},{17,1},{2,18},{18,2},{3,19},{19,3},{4,20},{20... | collective-permute-start | bytes 49160 | tf_op jit(solution)/shard_map/ppermute | solution.py:403
  37.7 1.3 %collective-permute-start.1 = (f32[2,16,128]{2,1,0:T(8,128)S(1)}, f32[2,16,128]{2,1,0:T(8,128)S(1)}, u32[]{:S(2)}, u32[]{:S(2)}) collective-permute-start(f32[2,16,128]{2,1,0:T(8,128)S(1)} %get-tuple-element.10.ends.old_ends), channel_id=1, source_target_pairs={{0,16},{16,0},{1,17},{17,1},{2,18},{18,2},{3,19},{19,3},{4,20},{20... | collective-permute-start | bytes 49160 | tf_op jit(solution)/shard_map/ppermute | solution.py:403
  39.0 40.2 %copy-start.2 = (f32[2,256,128]{2,1,0:T(8,128)S(1)}, f32[2,256,128]{2,1,0:T(8,128)}, u32[]{:S(2)}) copy-start(f32[2,256,128]{2,1,0:T(8,128)} %sources.3) | copy-start | bytes 786436
  39.1 40.2 %copy-start.3 = (f32[256,128]{1,0:T(8,128)S(1)}, f32[256,128]{1,0:T(8,128)}, u32[]{:S(2)}) copy-start(f32[256,128]{1,0:T(8,128)} %metric.3) | copy-start | bytes 393220
  39.1 40.2 %copy-start.4 = (f32[256,128]{1,0:T(8,128)S(1)}, f32[256,128]{1,0:T(8,128)}, u32[]{:S(2)}) copy-start(f32[256,128]{1,0:T(8,128)} %helm.3) | copy-start | bytes 393220

commit v8 on v7

--- a/solution.py
+++ b/solution.py
@@ -298,7 +298,7 @@
             wz, wh = weight * z1, weight * h
             for q, (one, two) in enumerate(((u1, z1), (u1, h), (g, z1), (g, h), (wz, z1), (wz, h), (wh, h))):
                 sums[q] += one * two
-            place = 130 * place_of(a // 8, a // 2 % 4) + 16 * chunk + a % 2
+            place = 130 * (a // 2) + 16 * chunk + a % 2
             sent[pl.ds(place, 8, stride=2), :] = before
             sent[pl.ds(place + 64, 8, stride=2), :] = new
     lane = lax.broadcasted_iota(jnp.int32, (2, LANES), 1)
@@ -332,7 +332,7 @@
     inverse = 1.0 / m
     weight = helm[...] * inverse - SHIFT * m
     for f in range(2):
-        mine = jnp.where(row % 2 == f, every, 0.0)
+        mine = jnp.where(row % 8 // 4 == f, every, 0.0)
         zeroth = jnp.sum(mine, axis=0, keepdims=True)
         n0, n1 = pick(zeroth, 7), pick(zeroth, 8)
         delta = n0 + n1
@@ -351,7 +351,7 @@
         for h in range(2):
             pair = []
             for field in range(2):
-                places = [130 * place_of(f, quarter) + 64 * field + h for quarter in range(4)]
+                places = [130 * (4 * f + quarter) + 64 * field + h for quarter in range(4)]
                 columns = [received[pl.ds(place, BLOCK, stride=2), :] for place in places]
                 pair.append(jnp.concatenate(columns, axis=0).T)
             old, new = pair
@@ -392,7 +392,7 @@
 
 def per_device(sources, metric, helm):
     table, waves = (jnp.asarray(a) for a in tables())
-    line, column = ("pair", "core", "half"), ("gy", "pair", "core")
+    line, column = ("half", "pair", "core"), ("gy", "pair", "core")
     here = lax.axis_index("gy") * lax.axis_size("pair") + lax.axis_index("pair")
     here = jnp.full((1, LANES), here, jnp.float32)
     core = jnp.full((1, LANES), lax.axis_index("core"), jnp.float32)
@@ -408,7 +408,7 @@
         [pltpu.VMEM(sources.shape, sources.dtype), block, block, pltpu.SemaphoreType.DMA((4,))],
         in_specs=[hbm] * 5 + [vmem] * 2,
     )(*far(sources, metric, helm, table, waves), here, core)
-    blocks = exchange(sent, line, 8, 128)
+    blocks = exchange(sent, ("pair", "core", "half"), 8, 128)
     first, ends = call(pencil_first, [SPECTRUM, ENDS], [RS])(blocks, table, waves)
     sibling = swap(ends)
     (sent,) = call(leave_lines, [SENT], [])(ends, sibling, waves, here, core)

time: 80.7 us -> 80.9 us (level)
  no operation moved by 1% of the time
where the time goes in v8:
time: 80.9 us; the launch traced here: 80.6 us
  blocking collectives  71.4 us (88%)
  Pallas kernels  5.68 us (7%)
  waiting for transfers between devices  1.93 us (2%)
    all_to_all x5, blocking collectives, exchange(): moved = lax.all_to_all(flat.reshape(*shape, LANES), axes, 0, 0, tiled=True)  71.4 us
    ppermute x2, waiting for transfers between devices, swap(): return lax.ppermute(ends, 'core', [(0, 1), (1, 0)])  1.93 us
  transfers between devices with their start and end apart: 2, of which 2 were waited for; matrix products, arithmetic and copies ran while one was open for 0% of the time, Pallas kernels for 0%

profile of v8, /device:TPU:0, one launch (start us, length us, event | category | flops | bytes accessed | tf_op | source)
XLA Modules:
  0.0 80.6 jit_solution(15055678931958205737)
XLA Ops:
  0.6 0.0 copy-start.1
  0.7 0.0 copy-start
  0.7 1.4 %shard_map.68 = f32[1024,128]{1,0:T(8,128)S(1)} custom-call(f32[2,256,128]{2,1,0:T(8,128)} %sources.3, f32[256,128]{1,0:T(8,128)} %metric.3, f32[256,128]{1,0:T(8,128)} %helm.3, bf16[16,2,256,256]{3,2,1,0:T(8,128)(2,1)} %constant.19.clone.table, f32[4,16,128]{2,1,0:T(8,128)} %constant.20.clone.waves, f32[1,128]{1,0:T(1,128)S(1)} %broadcast_in_dim.6.here, ...), custom_call_target="tpu_custom_call" | custom-call | tf_op jit(solution)/shard_map/pallas_call | solution.py:405
  2.1 14.7 %all_to_all.25 = f32[8,128,128]{2,1,0:T(8,128)S(1)} all-to-all(f32[8,128,128]{2,1,0:T(8,128)S(1)} %bitcast.16), channel_id=1, replica_groups=mesh['half'=2,'pair'=2,'core'=2,'gy'=16] {'pair','core','half'}, dimensions={0} | all-to-all | bytes 1048576 | tf_op jit(solution)/shard_map/all_to_all | solution.py:389
  16.8 0.0 copy-done.1
  16.8 0.0 copy-done
  16.8 0.6 shard_map.69
  17.4 0.6 collective-permute-start
  18.0 0.8 %collective-permute-done.sibling = f32[2,16,128]{2,1,0:T(8,128)S(1)} collective-permute-done((f32[2,16,128]{2,1,0:T(8,128)S(1)}, f32[2,16,128]{2,1,0:T(8,128)S(1)}, u32[]{:S(2)}, u32[]{:S(2)}) %collective-permute-start) | collective-permute-done | bytes 16416 | tf_op jit(solution)/shard_map/ppermute | solution.py:403
  18.9 17.5 %all_to_all.26 = f32[64,8,128]{2,1,0:T(8,128)S(1)} all-to-all(f32[64,8,128]{2,1,0:T(8,128)S(1)} %bitcast.19), channel_id=1, replica_groups=mesh['half'=2,'pair'=2,'core'=2,'gy'=16] {'gy','pair','core'}, dimensions={0} | all-to-all | bytes 524288 | tf_op jit(solution)/shard_map/all_to_all | solution.py:389
  36.4 1.3 %shard_map.71 = (f32[512,128]{1,0:T(8,128)S(1)}, f32[2,16,128]{2,1,0:T(8,128)S(1)}, f32[16,32,128]{2,1,0:T(8,128)S(1)}, f32[2,8,128]{2,1,0:T(8,128)S(1)}) custom-call(f32[512,128]{1,0:T(8,128)S(1)} %bitcast.18, f32[1024,128]{1,0:T(8,128)S(1)} %bitcast.11, f32[512,128]{1,0:T(8,128)S(1)} %get-tuple-element.9.old, ...), custom_call_target="tpu_custom_call" | custom-call | tf_op jit(solution)/shard_map/pallas_call | solution.py:416
  37.7 0.2 collective-permute-start.1
  37.9 1.1 %collective-permute-done.1.sibling = f32[2,16,128]{2,1,0:T(8,128)S(1)} collective-permute-done((f32[2,16,128]{2,1,0:T(8,128)S(1)}, f32[2,16,128]{2,1,0:T(8,128)S(1)}, u32[]{:S(2)}, u32[]{:S(2)}) %collective-permute-start.1) | collective-permute-done | bytes 16416 | tf_op jit(solution)/shard_map/ppermute | solution.py:403
  39.0 0.0 copy-start.2
  39.1 0.0 copy-start.3
  39.1 0.0 copy-start.4
  39.1 14.2 %all_to_all.27 = f32[64,8,128]{2,1,0:T(8,128)S(1)} all-to-all(f32[64,8,128]{2,1,0:T(8,128)S(1)} %bitcast.20), channel_id=1, replica_groups=mesh['half'=2,'pair'=2,'core'=2,'gy'=16] {'gy','pair','core'}, dimensions={0} | all-to-all | bytes 524288 | tf_op jit(solution)/shard_map/all_to_all | solution.py:389
  53.3 1.1 %shard_map.73 = f32[1040,128]{1,0:T(8,128)S(1)} custom-call(f32[512,128]{1,0:T(8,128)S(1)} %bitcast.17, f32[1024,128]{1,0:T(8,128)S(1)} %bitcast.12, f32[512,128]{1,0:T(8,128)S(1)} %get-tuple-element.11.old, f32[2,16,128]{2,1,0:T(8,128)S(1)} %get-tuple-element.10.ends.old_ends, f32[2,16,128]{2,1,0:T(8,128)S(1)} %collective-permute-done.1.sibling, ...), custom_call_target="tpu_custom_call" | custom-call | tf_op jit(solution)/shard_map/pallas_call | solution.py:422
  54.4 14.1 %all_to_all.28 = f32[8,65,2,128]{3,2,1,0:T(2,128)S(1)} all-to-all(f32[8,65,2,128]{3,2,1,0:T(2,128)S(1)} %bitcast.15), channel_id=1, replica_groups=mesh['half'=2,'pair'=2,'core'=2,'gy'=16] {'half','pair','core'}, dimensions={0} | all-to-all | bytes 1064960 | tf_op jit(solution)/shard_map/all_to_all | solution.py:389
  68.5 10.8 %all_to_all.29 = f32[16,8,128]{2,1,0:T(8,128)S(1)} all-to-all(f32[16,8,128]{2,1,0:T(8,128)S(1)} %bitcast.22), channel_id=1, replica_groups=mesh['half'=2,'pair'=2,'core'=2,'gy'=16] {'gy'}, dimensions={0} | all-to-all | bytes 131072 | tf_op jit(solution)/shard_map/all_to_all | solution.py:389
  79.4 0.0 copy-done.2
  79.4 0.0 copy-done.3
  79.4 0.0 copy-done.4
  79.4 1.2 %shard_map.75 = (f32[2,256,128]{2,1,0:T(8,128)}, f32[2,256,128]{2,1,0:T(8,128)}) custom-call(f32[1040,128]{1,0:T(8,128)S(1)} %bitcast.14, f32[128,128]{1,0:T(8,128)S(1)} %bitcast.21, f32[2,256,128]{2,1,0:T(8,128)S(1)} %copy-done.2, f32[256,128]{1,0:T(8,128)S(1)} %copy-done.3, f32[256,128]{1,0:T(8,128)S(1)} %copy-done.4), custom_call_target="tpu_custom_call" | custom-call | tf_op jit(solution)/shard_map/pallas_call | solution.py:428
  (5 shorter events, 0.1 us)
Async XLA Ops:
  0.6 16.2 %copy-start.1 = (f32[4,16,128]{2,1,0:T(8,128)S(1)}, f32[4,16,128]{2,1,0:T(8,128)}, u32[]{:S(2)}) copy-start(f32[4,16,128]{2,1,0:T(8,128)} %constant.20.clone.waves) | copy-start | bytes 98308
  0.7 16.1 %copy-start = (bf16[16,2,256,256]{3,2,1,0:T(8,128)(2,1)S(1)}, bf16[16,2,256,256]{3,2,1,0:T(8,128)(2,1)}, u32[]{:S(2)}) copy-start(bf16[16,2,256,256]{3,2,1,0:T(8,128)(2,1)} %constant.19.clone.table) | copy-start | bytes 12582916
  17.4 1.4 %collective-permute-start = (f32[2,16,128]{2,1,0:T(8,128)S(1)}, f32[2,16,128]{2,1,0:T(8,128)S(1)}, u32[]{:S(2)}, u32[]{:S(2)}) collective-permute-start(f32[2,16,128]{2,1,0:T(8,128)S(1)} %get-tuple-element.8.ends.old_ends), channel_id=1, source_target_pairs={{0,16},{16,0},{1,17},{17,1},{2,18},{18,2},{3,19},{19,3},{4,20},{20... | collective-permute-start | bytes 49160 | tf_op jit(solution)/shard_map/ppermute | solution.py:403
  37.7 1.3 %collective-permute-start.1 = (f32[2,16,128]{2,1,0:T(8,128)S(1)}, f32[2,16,128]{2,1,0:T(8,128)S(1)}, u32[]{:S(2)}, u32[]{:S(2)}) collective-permute-start(f32[2,16,128]{2,1,0:T(8,128)S(1)} %get-tuple-element.10.ends.old_ends), channel_id=1, source_target_pairs={{0,16},{16,0},{1,17},{17,1},{2,18},{18,2},{3,19},{19,3},{4,20},{20... | collective-permute-start | bytes 49160 | tf_op jit(solution)/shard_map/ppermute | solution.py:403
  39.0 40.3 %copy-start.2 = (f32[2,256,128]{2,1,0:T(8,128)S(1)}, f32[2,256,128]{2,1,0:T(8,128)}, u32[]{:S(2)}) copy-start(f32[2,256,128]{2,1,0:T(8,128)} %sources.3) | copy-start | bytes 786436
  39.1 40.3 %copy-start.3 = (f32[256,128]{1,0:T(8,128)S(1)}, f32[256,128]{1,0:T(8,128)}, u32[]{:S(2)}) copy-start(f32[256,128]{1,0:T(8,128)} %metric.3) | copy-start | bytes 393220
  39.1 40.3 %copy-start.4 = (f32[256,128]{1,0:T(8,128)S(1)}, f32[256,128]{1,0:T(8,128)}, u32[]{:S(2)}) copy-start(f32[256,128]{1,0:T(8,128)} %helm.3) | copy-start | bytes 393220

commit v9 on v7

--- a/solution.py
+++ b/solution.py
@@ -152,7 +152,7 @@
     moves = [(metric, metric_here), (helm, helm_here), (sources, source_here)]
     copies = [pltpu.make_async_copy(a, b, arrived.at[n]) for n, (a, b) in enumerate(moves)]
     for copy in copies:
-        copy.start()
+        copy.start(priority=1)
     copies[0].wait()
     inverse = 1.0 / metric_here[...]
     copies[1].wait()

time: 80.7 us -> 80.7 us (level)
  no operation moved by 1% of the time
where the time goes in v9:
time: 80.7 us; the launch traced here: 80.4 us
  blocking collectives  71.3 us (88%)
  Pallas kernels  5.68 us (7%)
  waiting for transfers between devices  1.93 us (2%)
    all_to_all x5, blocking collectives, exchange(): moved = lax.all_to_all(flat.reshape(*shape, LANES), axes, 0, 0, tiled=True)  71.3 us
    ppermute x2, waiting for transfers between devices, swap(): return lax.ppermute(ends, 'core', [(0, 1), (1, 0)])  1.93 us
  transfers between devices with their start and end apart: 2, of which 2 were waited for; matrix products, arithmetic and copies ran while one was open for 0% of the time, Pallas kernels for 0%

profile of v9, /device:TPU:0, one launch (start us, length us, event | category | flops | bytes accessed | tf_op | source)
XLA Modules:
  0.0 80.4 jit_solution(6808343058150262176)
XLA Ops:
  0.6 0.0 copy-start.1
  0.7 0.0 copy-start
  0.7 1.4 %shard_map.68 = f32[1024,128]{1,0:T(8,128)S(1)} custom-call(f32[2,256,128]{2,1,0:T(8,128)} %sources.3, f32[256,128]{1,0:T(8,128)} %metric.3, f32[256,128]{1,0:T(8,128)} %helm.3, bf16[16,2,256,256]{3,2,1,0:T(8,128)(2,1)} %constant.19.clone.table, f32[4,16,128]{2,1,0:T(8,128)} %constant.20.clone.waves, f32[1,128]{1,0:T(1,128)S(1)} %broadcast_in_dim.6.here, ...), custom_call_target="tpu_custom_call" | custom-call | tf_op jit(solution)/shard_map/pallas_call | solution.py:405
  2.1 14.7 %all_to_all.25 = f32[8,128,128]{2,1,0:T(8,128)S(1)} all-to-all(f32[8,128,128]{2,1,0:T(8,128)S(1)} %bitcast.16), channel_id=1, replica_groups=mesh['half'=2,'pair'=2,'core'=2,'gy'=16] {'pair','core','half'}, dimensions={0} | all-to-all | bytes 1048576 | tf_op jit(solution)/shard_map/all_to_all | solution.py:389
  16.8 0.0 copy-done.1
  16.8 0.0 copy-done
  16.8 0.6 shard_map.69
  17.4 0.6 collective-permute-start
  18.0 0.8 %collective-permute-done.sibling = f32[2,16,128]{2,1,0:T(8,128)S(1)} collective-permute-done((f32[2,16,128]{2,1,0:T(8,128)S(1)}, f32[2,16,128]{2,1,0:T(8,128)S(1)}, u32[]{:S(2)}, u32[]{:S(2)}) %collective-permute-start) | collective-permute-done | bytes 16416 | tf_op jit(solution)/shard_map/ppermute | solution.py:403
  18.9 17.5 %all_to_all.26 = f32[64,8,128]{2,1,0:T(8,128)S(1)} all-to-all(f32[64,8,128]{2,1,0:T(8,128)S(1)} %bitcast.19), channel_id=1, replica_groups=mesh['half'=2,'pair'=2,'core'=2,'gy'=16] {'gy','pair','core'}, dimensions={0} | all-to-all | bytes 524288 | tf_op jit(solution)/shard_map/all_to_all | solution.py:389
  36.4 1.3 %shard_map.71 = (f32[512,128]{1,0:T(8,128)S(1)}, f32[2,16,128]{2,1,0:T(8,128)S(1)}, f32[16,32,128]{2,1,0:T(8,128)S(1)}, f32[2,8,128]{2,1,0:T(8,128)S(1)}) custom-call(f32[512,128]{1,0:T(8,128)S(1)} %bitcast.18, f32[1024,128]{1,0:T(8,128)S(1)} %bitcast.11, f32[512,128]{1,0:T(8,128)S(1)} %get-tuple-element.9.old, ...), custom_call_target="tpu_custom_call" | custom-call | tf_op jit(solution)/shard_map/pallas_call | solution.py:416
  37.7 0.2 collective-permute-start.1
  37.9 1.1 %collective-permute-done.1.sibling = f32[2,16,128]{2,1,0:T(8,128)S(1)} collective-permute-done((f32[2,16,128]{2,1,0:T(8,128)S(1)}, f32[2,16,128]{2,1,0:T(8,128)S(1)}, u32[]{:S(2)}, u32[]{:S(2)}) %collective-permute-start.1) | collective-permute-done | bytes 16416 | tf_op jit(solution)/shard_map/ppermute | solution.py:403
  39.0 0.0 copy-start.2
  39.1 0.0 copy-start.3
  39.1 0.0 copy-start.4
  39.1 14.2 %all_to_all.27 = f32[64,8,128]{2,1,0:T(8,128)S(1)} all-to-all(f32[64,8,128]{2,1,0:T(8,128)S(1)} %bitcast.20), channel_id=1, replica_groups=mesh['half'=2,'pair'=2,'core'=2,'gy'=16] {'gy','pair','core'}, dimensions={0} | all-to-all | bytes 524288 | tf_op jit(solution)/shard_map/all_to_all | solution.py:389
  53.3 1.1 %shard_map.73 = f32[1040,128]{1,0:T(8,128)S(1)} custom-call(f32[512,128]{1,0:T(8,128)S(1)} %bitcast.17, f32[1024,128]{1,0:T(8,128)S(1)} %bitcast.12, f32[512,128]{1,0:T(8,128)S(1)} %get-tuple-element.11.old, f32[2,16,128]{2,1,0:T(8,128)S(1)} %get-tuple-element.10.ends.old_ends, f32[2,16,128]{2,1,0:T(8,128)S(1)} %collective-permute-done.1.sibling, ...), custom_call_target="tpu_custom_call" | custom-call | tf_op jit(solution)/shard_map/pallas_call | solution.py:422
  54.4 14.0 %all_to_all.28 = f32[8,65,2,128]{3,2,1,0:T(2,128)S(1)} all-to-all(f32[8,65,2,128]{3,2,1,0:T(2,128)S(1)} %bitcast.15), channel_id=1, replica_groups=mesh['half'=2,'pair'=2,'core'=2,'gy'=16] {'pair','core','half'}, dimensions={0} | all-to-all | bytes 1064960 | tf_op jit(solution)/shard_map/all_to_all | solution.py:389
  68.4 10.8 %all_to_all.29 = f32[16,8,128]{2,1,0:T(8,128)S(1)} all-to-all(f32[16,8,128]{2,1,0:T(8,128)S(1)} %bitcast.22), channel_id=1, replica_groups=mesh['half'=2,'pair'=2,'core'=2,'gy'=16] {'gy'}, dimensions={0} | all-to-all | bytes 131072 | tf_op jit(solution)/shard_map/all_to_all | solution.py:389
  79.2 0.0 copy-done.2
  79.2 0.0 copy-done.3
  79.2 0.0 copy-done.4
  79.3 1.2 %shard_map.75 = (f32[2,256,128]{2,1,0:T(8,128)}, f32[2,256,128]{2,1,0:T(8,128)}) custom-call(f32[1040,128]{1,0:T(8,128)S(1)} %bitcast.14, f32[128,128]{1,0:T(8,128)S(1)} %bitcast.21, f32[2,256,128]{2,1,0:T(8,128)S(1)} %copy-done.2, f32[256,128]{1,0:T(8,128)S(1)} %copy-done.3, f32[256,128]{1,0:T(8,128)S(1)} %copy-done.4), custom_call_target="tpu_custom_call" | custom-call | tf_op jit(solution)/shard_map/pallas_call | solution.py:428
  (5 shorter events, 0.1 us)
Async XLA Ops:
  0.6 16.2 %copy-start.1 = (f32[4,16,128]{2,1,0:T(8,128)S(1)}, f32[4,16,128]{2,1,0:T(8,128)}, u32[]{:S(2)}) copy-start(f32[4,16,128]{2,1,0:T(8,128)} %constant.20.clone.waves) | copy-start | bytes 98308
  0.7 16.1 %copy-start = (bf16[16,2,256,256]{3,2,1,0:T(8,128)(2,1)S(1)}, bf16[16,2,256,256]{3,2,1,0:T(8,128)(2,1)}, u32[]{:S(2)}) copy-start(bf16[16,2,256,256]{3,2,1,0:T(8,128)(2,1)} %constant.19.clone.table) | copy-start | bytes 12582916
  17.4 1.4 %collective-permute-start = (f32[2,16,128]{2,1,0:T(8,128)S(1)}, f32[2,16,128]{2,1,0:T(8,128)S(1)}, u32[]{:S(2)}, u32[]{:S(2)}) collective-permute-start(f32[2,16,128]{2,1,0:T(8,128)S(1)} %get-tuple-element.8.ends.old_ends), channel_id=1, source_target_pairs={{0,16},{16,0},{1,17},{17,1},{2,18},{18,2},{3,19},{19,3},{4,20},{20... | collective-permute-start | bytes 49160 | tf_op jit(solution)/shard_map/ppermute | solution.py:403
  37.7 1.3 %collective-permute-start.1 = (f32[2,16,128]{2,1,0:T(8,128)S(1)}, f32[2,16,128]{2,1,0:T(8,128)S(1)}, u32[]{:S(2)}, u32[]{:S(2)}) collective-permute-start(f32[2,16,128]{2,1,0:T(8,128)S(1)} %get-tuple-element.10.ends.old_ends), channel_id=1, source_target_pairs={{0,16},{16,0},{1,17},{17,1},{2,18},{18,2},{3,19},{19,3},{4,20},{20... | collective-permute-start | bytes 49160 | tf_op jit(solution)/shard_map/ppermute | solution.py:403
  39.0 40.2 %copy-start.2 = (f32[2,256,128]{2,1,0:T(8,128)S(1)}, f32[2,256,128]{2,1,0:T(8,128)}, u32[]{:S(2)}) copy-start(f32[2,256,128]{2,1,0:T(8,128)} %sources.3) | copy-start | bytes 786436
  39.1 40.2 %copy-start.3 = (f32[256,128]{1,0:T(8,128)S(1)}, f32[256,128]{1,0:T(8,128)}, u32[]{:S(2)}) copy-start(f32[256,128]{1,0:T(8,128)} %metric.3) | copy-start | bytes 393220
  39.1 40.2 %copy-start.4 = (f32[256,128]{1,0:T(8,128)S(1)}, f32[256,128]{1,0:T(8,128)}, u32[]{:S(2)}) copy-start(f32[256,128]{1,0:T(8,128)} %helm.3) | copy-start | bytes 393220

commit v10 on v7

--- a/solution.py
+++ b/solution.py
@@ -193,12 +193,15 @@
 
 def local_sums(spectrum, waves, ends):
     rho = waves[0]
-    p = lines(spectrum, 0)
-    q = lines(spectrum, BLOCK - 1)
-    for y in range(1, BLOCK):
-        p = rho * p + lines(spectrum, y)
-        q = rho * q + lines(spectrum, BLOCK - 1 - y)
-    ends[0], ends[1] = p, q
+    part = BLOCK // 2
+    p = [lines(spectrum, 0), lines(spectrum, part)]
+    q = [lines(spectrum, part - 1), lines(spectrum, BLOCK - 1)]
+    for y in range(1, part):
+        for n in range(2):
+            p[n] = rho * p[n] + lines(spectrum, part * n + y)
+            q[n] = rho * q[n] + lines(spectrum, part * (n + 1) - 1 - y)
+    through = jnp.exp(-0.5 * waves[1])
+    ends[0], ends[1] = p[1] + through * p[0], q[0] + through * q[1]
 
 
 def both_cores(ends, sibling, whole, upper):

time: 80.7 us -> 80.7 us (level)
  no operation moved by 1% of the time
where the time goes in v10:
time: 80.7 us; the launch traced here: 80.4 us
  blocking collectives  71.3 us (88%)
  Pallas kernels  5.63 us (7%)
  waiting for transfers between devices  1.94 us (2%)
    all_to_all x5, blocking collectives, exchange(): moved = lax.all_to_all(flat.reshape(*shape, LANES), axes, 0, 0, tiled=True)  71.3 us
    ppermute x2, waiting for transfers between devices, swap(): return lax.ppermute(ends, 'core', [(0, 1), (1, 0)])  1.94 us
  transfers between devices with their start and end apart: 2, of which 2 were waited for; matrix products, arithmetic and copies ran while one was open for 0% of the time, Pallas kernels for 0%

profile of v10, /device:TPU:0, one launch (start us, length us, event | category | flops | bytes accessed | tf_op | source)
XLA Modules:
  0.0 80.4 jit_solution(9254150373855596929)
XLA Ops:
  0.6 0.0 copy-start.1
  0.7 0.0 copy-start
  0.7 1.4 %shard_map.68 = f32[1024,128]{1,0:T(8,128)S(1)} custom-call(f32[2,256,128]{2,1,0:T(8,128)} %sources.3, f32[256,128]{1,0:T(8,128)} %metric.3, f32[256,128]{1,0:T(8,128)} %helm.3, bf16[16,2,256,256]{3,2,1,0:T(8,128)(2,1)} %constant.19.clone.table, f32[4,16,128]{2,1,0:T(8,128)} %constant.20.clone.waves, f32[1,128]{1,0:T(1,128)S(1)} %broadcast_in_dim.6.here, ...), custom_call_target="tpu_custom_call" | custom-call | tf_op jit(solution)/shard_map/pallas_call | solution.py:408
  2.1 14.7 %all_to_all.25 = f32[8,128,128]{2,1,0:T(8,128)S(1)} all-to-all(f32[8,128,128]{2,1,0:T(8,128)S(1)} %bitcast.16), channel_id=1, replica_groups=mesh['half'=2,'pair'=2,'core'=2,'gy'=16] {'pair','core','half'}, dimensions={0} | all-to-all | bytes 1048576 | tf_op jit(solution)/shard_map/all_to_all | solution.py:392
  16.8 0.0 copy-done.1
  16.8 0.0 copy-done
  16.8 0.6 shard_map.69
  17.4 0.6 collective-permute-start
  18.0 0.8 %collective-permute-done.sibling = f32[2,16,128]{2,1,0:T(8,128)S(1)} collective-permute-done((f32[2,16,128]{2,1,0:T(8,128)S(1)}, f32[2,16,128]{2,1,0:T(8,128)S(1)}, u32[]{:S(2)}, u32[]{:S(2)}) %collective-permute-start) | collective-permute-done | bytes 16416 | tf_op jit(solution)/shard_map/ppermute | solution.py:406
  18.8 17.5 %all_to_all.26 = f32[64,8,128]{2,1,0:T(8,128)S(1)} all-to-all(f32[64,8,128]{2,1,0:T(8,128)S(1)} %bitcast.19), channel_id=1, replica_groups=mesh['half'=2,'pair'=2,'core'=2,'gy'=16] {'gy','pair','core'}, dimensions={0} | all-to-all | bytes 524288 | tf_op jit(solution)/shard_map/all_to_all | solution.py:392
  36.4 1.3 %shard_map.71 = (f32[512,128]{1,0:T(8,128)S(1)}, f32[2,16,128]{2,1,0:T(8,128)S(1)}, f32[16,32,128]{2,1,0:T(8,128)S(1)}, f32[2,8,128]{2,1,0:T(8,128)S(1)}) custom-call(f32[512,128]{1,0:T(8,128)S(1)} %bitcast.18, f32[1024,128]{1,0:T(8,128)S(1)} %bitcast.11, f32[512,128]{1,0:T(8,128)S(1)} %get-tuple-element.9.old, ...), custom_call_target="tpu_custom_call" | custom-call | tf_op jit(solution)/shard_map/pallas_call | solution.py:419
  37.7 0.2 collective-permute-start.1
  37.9 1.1 %collective-permute-done.1.sibling = f32[2,16,128]{2,1,0:T(8,128)S(1)} collective-permute-done((f32[2,16,128]{2,1,0:T(8,128)S(1)}, f32[2,16,128]{2,1,0:T(8,128)S(1)}, u32[]{:S(2)}, u32[]{:S(2)}) %collective-permute-start.1) | collective-permute-done | bytes 16416 | tf_op jit(solution)/shard_map/ppermute | solution.py:406
  39.0 0.0 copy-start.2
  39.0 0.0 copy-start.3
  39.0 0.0 copy-start.4
  39.0 14.2 %all_to_all.27 = f32[64,8,128]{2,1,0:T(8,128)S(1)} all-to-all(f32[64,8,128]{2,1,0:T(8,128)S(1)} %bitcast.20), channel_id=1, replica_groups=mesh['half'=2,'pair'=2,'core'=2,'gy'=16] {'gy','pair','core'}, dimensions={0} | all-to-all | bytes 524288 | tf_op jit(solution)/shard_map/all_to_all | solution.py:392
  53.3 1.1 %shard_map.73 = f32[1040,128]{1,0:T(8,128)S(1)} custom-call(f32[512,128]{1,0:T(8,128)S(1)} %bitcast.17, f32[1024,128]{1,0:T(8,128)S(1)} %bitcast.12, f32[512,128]{1,0:T(8,128)S(1)} %get-tuple-element.11.old, f32[2,16,128]{2,1,0:T(8,128)S(1)} %get-tuple-element.10.ends.old_ends, f32[2,16,128]{2,1,0:T(8,128)S(1)} %collective-permute-done.1.sibling, ...), custom_call_target="tpu_custom_call" | custom-call | tf_op jit(solution)/shard_map/pallas_call | solution.py:425
  54.3 14.0 %all_to_all.28 = f32[8,65,2,128]{3,2,1,0:T(2,128)S(1)} all-to-all(f32[8,65,2,128]{3,2,1,0:T(2,128)S(1)} %bitcast.15), channel_id=1, replica_groups=mesh['half'=2,'pair'=2,'core'=2,'gy'=16] {'pair','core','half'}, dimensions={0} | all-to-all | bytes 1064960 | tf_op jit(solution)/shard_map/all_to_all | solution.py:392
  68.3 10.8 %all_to_all.29 = f32[16,8,128]{2,1,0:T(8,128)S(1)} all-to-all(f32[16,8,128]{2,1,0:T(8,128)S(1)} %bitcast.22), channel_id=1, replica_groups=mesh['half'=2,'pair'=2,'core'=2,'gy'=16] {'gy'}, dimensions={0} | all-to-all | bytes 131072 | tf_op jit(solution)/shard_map/all_to_all | solution.py:392
  79.2 0.0 copy-done.2
  79.2 0.0 copy-done.3
  79.2 0.0 copy-done.4
  79.2 1.2 %shard_map.75 = (f32[2,256,128]{2,1,0:T(8,128)}, f32[2,256,128]{2,1,0:T(8,128)}) custom-call(f32[1040,128]{1,0:T(8,128)S(1)} %bitcast.14, f32[128,128]{1,0:T(8,128)S(1)} %bitcast.21, f32[2,256,128]{2,1,0:T(8,128)S(1)} %copy-done.2, f32[256,128]{1,0:T(8,128)S(1)} %copy-done.3, f32[256,128]{1,0:T(8,128)S(1)} %copy-done.4), custom_call_target="tpu_custom_call" | custom-call | tf_op jit(solution)/shard_map/pallas_call | solution.py:431
  (5 shorter events, 0.1 us)
Async XLA Ops:
  0.6 16.2 %copy-start.1 = (f32[4,16,128]{2,1,0:T(8,128)S(1)}, f32[4,16,128]{2,1,0:T(8,128)}, u32[]{:S(2)}) copy-start(f32[4,16,128]{2,1,0:T(8,128)} %constant.20.clone.waves) | copy-start | bytes 98308
  0.7 16.1 %copy-start = (bf16[16,2,256,256]{3,2,1,0:T(8,128)(2,1)S(1)}, bf16[16,2,256,256]{3,2,1,0:T(8,128)(2,1)}, u32[]{:S(2)}) copy-start(bf16[16,2,256,256]{3,2,1,0:T(8,128)(2,1)} %constant.19.clone.table) | copy-start | bytes 12582916
  17.4 1.4 %collective-permute-start = (f32[2,16,128]{2,1,0:T(8,128)S(1)}, f32[2,16,128]{2,1,0:T(8,128)S(1)}, u32[]{:S(2)}, u32[]{:S(2)}) collective-permute-start(f32[2,16,128]{2,1,0:T(8,128)S(1)} %get-tuple-element.8.ends.old_ends), channel_id=1, source_target_pairs={{0,16},{16,0},{1,17},{17,1},{2,18},{18,2},{3,19},{19,3},{4,20},{20... | collective-permute-start | bytes 49160 | tf_op jit(solution)/shard_map/ppermute | solution.py:406
  37.7 1.3 %collective-permute-start.1 = (f32[2,16,128]{2,1,0:T(8,128)S(1)}, f32[2,16,128]{2,1,0:T(8,128)S(1)}, u32[]{:S(2)}, u32[]{:S(2)}) collective-permute-start(f32[2,16,128]{2,1,0:T(8,128)S(1)} %get-tuple-element.10.ends.old_ends), channel_id=1, source_target_pairs={{0,16},{16,0},{1,17},{17,1},{2,18},{18,2},{3,19},{19,3},{4,20},{20... | collective-permute-start | bytes 49160 | tf_op jit(solution)/shard_map/ppermute | solution.py:406
  39.0 40.2 %copy-start.2 = (f32[2,256,128]{2,1,0:T(8,128)S(1)}, f32[2,256,128]{2,1,0:T(8,128)}, u32[]{:S(2)}) copy-start(f32[2,256,128]{2,1,0:T(8,128)} %sources.3) | copy-start | bytes 786436
  39.0 40.2 %copy-start.3 = (f32[256,128]{1,0:T(8,128)S(1)}, f32[256,128]{1,0:T(8,128)}, u32[]{:S(2)}) copy-start(f32[256,128]{1,0:T(8,128)} %metric.3) | copy-start | bytes 393220
  39.0 40.2 %copy-start.4 = (f32[256,128]{1,0:T(8,128)S(1)}, f32[256,128]{1,0:T(8,128)}, u32[]{:S(2)}) copy-start(f32[256,128]{1,0:T(8,128)} %helm.3) | copy-start | bytes 393220
